TPU v7x, 32 devices: a whole 2x2x4 slice. The times are simulated.
32 devices in a mesh: heads: 4 (over z), seq: 8 (over y, x, core).
Axes of the slice: x: 2, y: 2, z: 4, core: 2. Of those that a mesh axis runs over, the one named last changes fastest.
Arguments:
- frames: bfloat16 [8, 1024, 1152], P('seq', None, 'heads'), may hold values from -6 to 6
- qkv_spatial: bfloat16 [3, 1152, 1152], P(None, None, 'heads'), may hold values from -1 to 1
- out_spatial: bfloat16 [1152, 1152], P('heads'), may hold values from -0.1875 to 0.1875
- qkv_temporal: bfloat16 [3, 1152, 1152], P(None, None, 'heads'), may hold values from -1 to 1
- out_temporal: bfloat16 [1152, 1152], P('heads'), may hold values from -0.1875 to 0.1875
- spatial_mask: int32 [8, 8, 8], P('seq'), may hold values from 0 to 1
- temporal_mask: int32 [8, 8, 8], replicated, may hold values 0 or 1
- cotangent: bfloat16 [8, 1024, 1152], P(None, 'seq', 'heads'), may hold values from -6 to 6
Outputs:
- result: bfloat16 [8, 1024, 1152], P(None, 'seq', 'heads')
- frames_grad: bfloat16 [8, 1024, 1152], P('seq', None, 'heads')
- spatial_qkv_grad: float32 [3, 1152, 1152], P(None, 'seq', 'heads')
- spatial_out_grad: float32 [1152, 1152], P('heads', 'seq')
- temporal_qkv_grad: float32 [3, 1152, 1152], P(None, 'seq', 'heads')
- temporal_out_grad: float32 [1152, 1152], P('heads', 'seq')
All inputs are finite; a program needn't handle non-finite values.
Results may differ from a plain program's by a relative error of at most 0.018.
Values may be sent and summed in bfloat16 or wider, within the bound.
A program may use at most 192 MiB of HBM per device.

v0:
```python
import jax
import jax.numpy as jnp
from jax import lax
from jax.sharding import PartitionSpec as P

HEAD_SIZE = 72


def row_features(share_rows):
    return lax.all_gather(share_rows, "heads", axis=1, tiled=True)


def relayout(block_rows):
    return lax.all_to_all(block_rows, "seq", split_axis=1, concat_axis=0, tiled=True)


def normalize(full_rows):
    values = full_rows.astype(jnp.float32)
    center = values - jnp.mean(values, axis=-1, keepdims=True)
    inverse = lax.rsqrt(jnp.mean(center * center, axis=-1, keepdims=True) + 1e-06)
    return (center * inverse, inverse)


def attention_probs(query_rows, key_matrix, allowed):
    logit_scores = jnp.einsum(
        "lbhd,mbhd->bhlm", query_rows, key_matrix, preferred_element_type=jnp.float32
    ) * HEAD_SIZE ** (-0.5)
    logit_scores = jnp.where(allowed[:, None], logit_scores, -1e30)
    weights = jnp.exp(logit_scores - jnp.max(logit_scores, axis=-1, keepdims=True))
    return weights / jnp.sum(weights, axis=-1, keepdims=True)


def attend_forward(query_rows, key_matrix, value_matrix, allowed):
    softmax_weights = attention_probs(query_rows, key_matrix, allowed)
    blended_rows = jnp.einsum(
        "bhlm,mbhd->lbhd",
        softmax_weights.astype(jnp.bfloat16),
        value_matrix,
        preferred_element_type=jnp.float32,
    )
    return blended_rows.astype(jnp.bfloat16)


def attend_backward(query_rows, key_matrix, value_matrix, allowed, grad_mixed):
    softmax_weights = attention_probs(query_rows, key_matrix, allowed)
    value_gradient = jnp.einsum(
        "bhlm,lbhd->mbhd",
        softmax_weights.astype(jnp.bfloat16),
        grad_mixed,
        preferred_element_type=jnp.float32,
    ).astype(jnp.bfloat16)
    probability_gradient = jnp.einsum(
        "lbhd,mbhd->bhlm", grad_mixed, value_matrix, preferred_element_type=jnp.float32
    )
    row_delta = jnp.sum(softmax_weights * probability_gradient, axis=-1, keepdims=True)
    score_gradient = (
        softmax_weights * (probability_gradient - row_delta) * HEAD_SIZE ** (-0.5)
    ).astype(jnp.bfloat16)
    query_gradient = jnp.einsum(
        "bhlm,mbhd->lbhd", score_gradient, key_matrix, preferred_element_type=jnp.float32
    ).astype(jnp.bfloat16)
    key_gradient = jnp.einsum(
        "bhlm,lbhd->mbhd", score_gradient, query_rows, preferred_element_type=jnp.float32
    ).astype(jnp.bfloat16)
    return (query_gradient, key_gradient, value_gradient)


def layer_forward(share_rows, qkv_weights, out_weights, allowed, length, batch_count):
    own_width = share_rows.shape[1]
    full_rows = row_features(share_rows)
    normed, inverse = normalize(full_rows)
    normed_low = normed.astype(jnp.bfloat16)
    projected = jnp.einsum(
        "nd,kde->kne", normed_low, qkv_weights, preferred_element_type=jnp.float32
    ).astype(jnp.bfloat16)
    shaped = projected.reshape(3, length, batch_count, own_width // HEAD_SIZE, HEAD_SIZE)
    blended_rows = attend_forward(shaped[0], shaped[1], shaped[2], allowed).reshape(
        length * batch_count, own_width
    )
    update = jnp.dot(blended_rows, out_weights, preferred_element_type=jnp.float32)
    summed = lax.psum_scatter(update, "heads", scatter_dimension=1, tiled=True)
    output = (share_rows.astype(jnp.float32) + summed).astype(jnp.bfloat16)
    return (output, (normed, inverse, normed_low, shaped, blended_rows))


def layer_backward(grad_share, qkv_weights, out_weights, allowed, saved_state):
    normed, inverse, normed_low, shaped, blended_rows = saved_state
    own_width = grad_share.shape[1]
    grad_rows = row_features(grad_share)
    out_grad = jnp.einsum("nk,nd->kd", blended_rows, grad_rows, preferred_element_type=jnp.float32)
    grad_mixed = jnp.einsum(
        "nd,kd->nk", grad_rows, out_weights, preferred_element_type=jnp.float32
    ).astype(jnp.bfloat16)
    grad_mixed = grad_mixed.reshape(shaped.shape[1:])
    query_gradient, key_gradient, value_gradient = attend_backward(
        shaped[0], shaped[1], shaped[2], allowed, grad_mixed
    )
    qkv_grads = jnp.stack([query_gradient, key_gradient, value_gradient]).reshape(3, -1, own_width)
    qkv_grad = jnp.einsum("nd,kne->kde", normed_low, qkv_grads, preferred_element_type=jnp.float32)
    partial_term = jnp.einsum(
        "kne,kde->nd", qkv_grads, qkv_weights, preferred_element_type=jnp.float32
    )
    whole_sum = lax.psum(partial_term, "heads")
    mean_first = jnp.mean(whole_sum, axis=-1, keepdims=True)
    mean_second = jnp.mean(whole_sum * normed, axis=-1, keepdims=True)
    full_grad = inverse * (whole_sum - mean_first - normed * mean_second)
    own_grad = lax.dynamic_slice_in_dim(
        full_grad, lax.axis_index("heads") * own_width, own_width, 1
    )
    grad_in = (grad_share.astype(jnp.float32) + own_grad).astype(jnp.bfloat16)
    return (grad_in, qkv_grad, out_grad)


def shards(
    frames,
    qkv_spatial,
    out_spatial,
    qkv_temporal,
    out_temporal,
    spatial_mask,
    temporal_mask,
    cotangent,
):
    length = frames.shape[1]
    own_width = frames.shape[2]
    frame_count = temporal_mask.shape[1]
    local_count = length // lax.axis_size("seq")
    block_count = spatial_mask.shape[1]
    block_size = length // block_count
    grid_mask = (
        jnp.broadcast_to(
            spatial_mask[0][:, None, :, None], (block_count, block_size, block_count, block_size)
        ).reshape(length, length)
        == 1
    )
    block_ids = jnp.arange(length) // block_size
    spatial_allowed = (grid_mask | (block_ids[:, None] == block_ids[None, :]))[None]
    positions = lax.axis_index("seq") * local_count + jnp.arange(local_count)
    chosen = (positions // block_size)[:, None] == jnp.arange(block_count)[None, :]
    picked = jnp.sum(jnp.where(chosen[:, :, None, None], temporal_mask[None], 0), axis=1)
    frame_ids = jnp.arange(frame_count)
    causal = (frame_ids[:, None] >= frame_ids[None, :])[None]
    diagonal = (frame_ids[:, None] == frame_ids[None, :])[None]
    temporal_allowed = causal & ((picked == 1) | diagonal)
    hidden, spatial_state = layer_forward(
        frames.reshape(length, own_width), qkv_spatial, out_spatial, spatial_allowed, length, 1
    )
    by_position = relayout(hidden.reshape(1, length, own_width))
    result, temporal_state = layer_forward(
        by_position.reshape(length, own_width),
        qkv_temporal,
        out_temporal,
        temporal_allowed,
        frame_count,
        local_count,
    )
    grad_position, temporal_qkv_grad, temporal_out_grad = layer_backward(
        cotangent.reshape(length, own_width),
        qkv_temporal,
        out_temporal,
        temporal_allowed,
        temporal_state,
    )
    hidden_grad = relayout(grad_position.reshape(1, length, own_width))
    frames_grad, spatial_qkv_grad, spatial_out_grad = layer_backward(
        hidden_grad.reshape(length, own_width),
        qkv_spatial,
        out_spatial,
        spatial_allowed,
        spatial_state,
    )
    reduced = (
        lax.psum_scatter(
            spatial_qkv_grad.astype(jnp.bfloat16), "seq", scatter_dimension=1, tiled=True
        ).astype(jnp.float32),
        lax.psum_scatter(
            spatial_out_grad.astype(jnp.bfloat16), "seq", scatter_dimension=1, tiled=True
        ).astype(jnp.float32),
        lax.psum_scatter(
            temporal_qkv_grad.astype(jnp.bfloat16), "seq", scatter_dimension=1, tiled=True
        ).astype(jnp.float32),
        lax.psum_scatter(
            temporal_out_grad.astype(jnp.bfloat16), "seq", scatter_dimension=1, tiled=True
        ).astype(jnp.float32),
    )
    return (
        result.reshape(frame_count, local_count, own_width),
        frames_grad.reshape(1, length, own_width),
        reduced[0],
        reduced[1],
        reduced[2],
        reduced[3],
    )


def solution(mesh):
    placed = (
        P("seq", None, "heads"),
        P(None, None, "heads"),
        P("heads", None),
        P(None, None, "heads"),
        P("heads", None),
        P("seq", None, None),
        P(),
        P(None, "seq", "heads"),
    )
    return jax.shard_map(
        shards,
        mesh=mesh,
        in_specs=placed,
        out_specs=(
            P(None, "seq", "heads"),
            P("seq", None, "heads"),
            P(None, "seq", "heads"),
            P("heads", "seq"),
            P(None, "seq", "heads"),
            P("heads", "seq"),
        ),
        check_vma=False,
    )
```

profile of v0, /device:TPU:0, one launch (start us, length us, event | category | flops | bytes accessed | tf_op | source)
XLA Modules:
  0.0 1051.7 jit_solution(88185695746655098)
XLA Ops:
  11.0 51.8 %all-gather.10.cloned.1.call-done = bf16[1,1024,1152]{1,2,0:T(8,128)(2,1)} async-done(((bf16[1,1024,288]{1,2,0:T(8,128)(2,1)}), bf16[1,1024,1152]{1,2,0:T(8,128)(2,1)}) %all-gather.10.cloned.1.call-update) | async-done | bytes 2359312 | tf_op jit(solution)/shard_map/all_gather | solution.py:10
  74.0 11.9 %fusion.128 = (f32[4,1024]{1,0:T(4,128)S(1)}, f32[4,1024,1024]{1,2,0:T(8,128)}) fusion(pred[1024,1024]{0,1:T(8,128)(4,1)} %bitcast_or_fusion, bf16[1024,4,72]{0,2,1:T(8,128)(2,1)S(1)} %bitcast.249, bf16[1024,4,72]{0,2,1:T(8,128)(2,1)} %bitcast.251), kind=kOutput, calls=%fused_computation.162 | convolution fusion | flops 620758016 | bytes 19021824 | tf_op jit(solution)/shard_map/sub | solution.py:29
  85.9 7.5 fusion.71
  100.7 81.3 %reduce-scatter.11.cloned.1.call-done = f32[1024,288]{0,1:T(8,128)} async-done(((f32[1024,1152]{0,1:T(8,128)}), f32[1024,288]{0,1:T(8,128)}) %reduce-scatter.11.cloned.1.call-update) | async-done | bytes 1179664 | tf_op jit(solution)/shard_map/reduce_scatter | solution.py:81
  189.5 7.5 reduce.8
  199.7 14.0 %all_to_all.8 = bf16[8,2,18432]{2,1,0:T(2,128)(2,1)} all-to-all(bf16[8,2,18432]{2,1,0:T(2,128)(2,1)S(1)} %reshape.360), channel_id=1, replica_groups=mesh['heads'=4,'seq'=8] {'seq'}, dimensions={0} | all-to-all | bytes 1179648 | tf_op jit(solution)/shard_map/all_to_all | solution.py:14
  225.5 9.7 all-gather.8.cloned.1.call-done
  240.1 46.4 %all-gather.12.cloned.1.call-done = bf16[1,1024,1152]{1,2,0:T(8,128)(2,1)} async-done(((bf16[1,1024,288]{1,2,0:T(8,128)(2,1)}), bf16[1,1024,1152]{1,2,0:T(8,128)(2,1)}) %all-gather.12.cloned.1.call-update) | async-done | bytes 2359312 | tf_op jit(solution)/shard_map/all_gather | solution.py:10
  318.1 6.3 fusion.59
  324.5 6.1 fusion.60
  353.8 170.9 %all-reduce.3.cloned.1.call-done = f32[1024,1152]{1,0:T(8,128)} async-done(((f32[1024,1152]{1,0:T(8,128)}), f32[1024,1152]{1,0:T(8,128)}) %all-reduce.3.cloned.1.call-update) | async-done | bytes 4718608 | tf_op jit(solution)/shard_map/psum | solution.py:103
  539.7 14.0 %all_to_all.9 = bf16[8,2,18432]{2,1,0:T(2,128)(2,1)} all-to-all(bf16[8,2,18432]{2,1,0:T(2,128)(2,1)S(1)} %reshape.362), channel_id=1, replica_groups=mesh['heads'=4,'seq'=8] {'seq'}, dimensions={0} | all-to-all | bytes 1179648 | tf_op jit(solution)/shard_map/all_to_all | solution.py:14
  581.5 7.4 reshape.358
  593.8 15.7 %all-gather.14.cloned.1.call-done = bf16[1,1024,1152]{1,2,0:T(8,128)(2,1)} async-done(((bf16[1,1024,288]{1,2,0:T(8,128)(2,1)}), bf16[1,1024,1152]{1,2,0:T(8,128)(2,1)}) %all-gather.14.cloned.1.call-update) | async-done | bytes 2359312 | tf_op jit(solution)/shard_map/all_gather | solution.py:10
  614.6 8.3 fusion.132
  623.0 8.5 fusion.74
  631.6 22.7 %fusion.62 = bf16[4,72,1024]{2,1,0:T(8,128)(2,1)S(1)} fusion(bf16[1024,4,72]{0,2,1:T(8,128)(2,1)S(1)} %bitcast.252, f32[4,1024,1024]{1,2,0:T(8,128)} %fusion.132, f32[4,1024,1024]{1,2,0:T(8,128)} %get-tuple-element.55, f32[4,1024]{1,0:T(4,128)S(1)} %get-tuple-element.54), kind=kOutput, calls=%fused_computation.82 | convolution fusion | flops 633639936 | bytes 34750464 | tf_op jit(solution)/shard_map/bhlm,mbhd->lbhd/dot_general | solution.py:59
  654.3 24.4 %fusion.65 = bf16[4,72,1024]{2,1,0:T(8,128)(2,1)} fusion(bf16[1024,4,72]{0,2,1:T(8,128)(2,1)S(1)} %bitcast.250, f32[4,1024,1024]{1,2,0:T(8,128)} %fusion.132, f32[4,1024,1024]{1,2,0:T(8,128)} %get-tuple-element.55, f32[4,1024]{1,0:T(4,128)S(1)} %get-tuple-element.54), kind=kOutput, calls=%fused_computation.83 | convolution fusion | flops 633639936 | bytes 34750464 | tf_op jit(solution)/shard_map/bhlm,lbhd->mbhd/dot_general | solution.py:62
  688.2 7.6 reshape.356
  695.9 6.1 convolution_bitcast_fusion
  706.9 72.0 %reduce-scatter.13.cloned.1.call-done = f32[1024,288]{0,1:T(8,128)} async-done(((f32[1024,1152]{0,1:T(8,128)}), f32[1024,288]{0,1:T(8,128)}) %reduce-scatter.13.cloned.1.call-update) | async-done | bytes 1179664 | tf_op jit(solution)/shard_map/reduce_scatter | solution.py:81
  781.1 36.5 %reduce-scatter.15.cloned.1.call-done = bf16[288,144]{0,1:T(8,128)(2,1)} async-done(((bf16[288,1152]{0,1:T(8,128)(2,1)}), bf16[288,144]{0,1:T(8,128)(2,1)}) %reduce-scatter.15.cloned.1.call-update) | async-done | bytes 82960 | tf_op jit(solution)/shard_map/reduce_scatter | solution.py:176
  819.2 43.0 %reduce-scatter.19.cloned.1.call-done = bf16[144,864]{1,0:T(8,128)(2,1)} async-done(((bf16[1152,864]{1,0:T(8,128)(2,1)}), bf16[144,864]{1,0:T(8,128)(2,1)}) %reduce-scatter.19.cloned.1.call-update) | async-done | bytes 248848
  865.1 171.2 %all-reduce.5.cloned.1.call-done = f32[1024,1152]{1,0:T(8,128)} async-done(((f32[1024,1152]{1,0:T(8,128)}), f32[1024,1152]{1,0:T(8,128)}) %all-reduce.5.cloned.1.call-update) | async-done | bytes 4718608 | tf_op jit(solution)/shard_map/psum | solution.py:103
  (181 shorter events, 185.8 us)
Async XLA Ops:
  7.2 286.9 %copy-start = (bf16[3,1152,288]{1,2,0:T(8,128)(2,1)S(1)}, bf16[3,1152,288]{1,2,0:T(8,128)(2,1)}, u32[]{:S(2)}) copy-start(bf16[3,1152,288]{1,2,0:T(8,128)(2,1)} %param.11) | copy-start | bytes 5971972
  7.2 55.6 %all-gather.10.cloned.1.call-start = ((), (), s32[]{:S(2)}) async-start(), calls=%async_computation.15 | async-start | bytes 2949120 | tf_op jit(solution)/shard_map/all_gather | solution.py:10
  7.9 174.1 %reduce-scatter.11.cloned.1.call-start = ((), (), s32[]{:S(2)}) async-start(), calls=%async_computation.8 | async-start | bytes 5898240 | tf_op jit(solution)/shard_map/reduce_scatter | solution.py:81
  74.0 11.9 %copy-start.18 = (bf16[1,1024,288]{1,2,0:T(8,128)(2,1)}, bf16[1,1024,288]{1,2,0:T(8,128)(2,1)S(1)}, u32[]{:S(2)}) copy-start(bf16[1,1024,288]{1,2,0:T(8,128)(2,1)S(1)} %get-tuple-element.52) | copy-start | bytes 1769476
  74.0 11.9 %copy-start.8 = (bf16[1,1024,288]{1,2,0:T(8,128)(2,1)}, bf16[1,1024,288]{1,2,0:T(8,128)(2,1)S(1)}, u32[]{:S(2)}) copy-start(bf16[1,1024,288]{1,2,0:T(8,128)(2,1)S(1)} %get-tuple-element.53) | copy-start | bytes 1769476
  97.8 84.2 %copy-start.11 = (bf16[1,1024,288]{1,2,0:T(8,128)(2,1)S(1)}, bf16[1,1024,288]{1,2,0:T(8,128)(2,1)}, u32[]{:S(2)}) copy-start(bf16[1,1024,288]{1,2,0:T(8,128)(2,1)} %param.8) | copy-start | bytes 1769476
  97.8 137.4 %all-gather.8.cloned.1.call-start = ((), (), s32[]{:S(2)}) async-start(), calls=%async_computation.10 | async-start | bytes 2949120 | tf_op jit(solution)/shard_map/all_gather | solution.py:10
  100.5 186.1 %all-gather.12.cloned.1.call-start = ((), (), s32[]{:S(2)}) async-start(), calls=%async_computation.16 | async-start | bytes 2949120 | tf_op jit(solution)/shard_map/all_gather | solution.py:10
  213.7 21.5 %copy-start.16 = (bf16[288,1152]{1,0:T(8,128)(2,1)S(1)}, bf16[288,1152]{1,0:T(8,128)(2,1)}, u32[]{:S(2)}) copy-start(bf16[288,1152]{1,0:T(8,128)(2,1)} %param.12) | copy-start | bytes 1990660
  224.3 300.5 %all-reduce.3.cloned.1.call-start = ((), (), s32[]{:S(2)}) async-start(), calls=%async_computation.11 | async-start | bytes 9437184 | tf_op jit(solution)/shard_map/psum | solution.py:103
  318.1 12.5 %copy-start.31 = (f32[128,4,8]{2,1,0:T(4,128)}, f32[128,4,8]{2,1,0:T(4,128)S(1)}, u32[]{:S(2)}) copy-start(f32[128,4,8]{2,1,0:T(4,128)S(1)} %get-tuple-element.56) | copy-start | bytes 49156
  353.8 255.7 %all-gather.14.cloned.1.call-start = ((), (), s32[]{:S(2)}) async-start(), calls=%async_computation.17 | async-start | bytes 2949120 | tf_op jit(solution)/shard_map/all_gather | solution.py:10
  561.7 140.4 %reduce-scatter.17.cloned.1.call-start = ((), (), s32[]{:S(2)}) async-start(), calls=%async_computation.14 | async-start | bytes 995328 | tf_op jit(solution)/shard_map/reduce_scatter | solution.py:182
  571.6 132.1 %reduce-scatter.21.cloned.1.call-start = ((), (), s32[]{:S(2)}) async-start(), calls=%async_computation.19 | async-start | bytes 2322432
  589.0 189.9 %reduce-scatter.13.cloned.1.call-start = ((), (), s32[]{:S(2)}) async-start(), calls=%async_computation.9 | async-start | bytes 5898240 | tf_op jit(solution)/shard_map/reduce_scatter | solution.py:81
  593.7 15.8 %copy-start.15 = (bf16[288,1152]{1,0:T(8,128)(2,1)S(1)}, bf16[288,1152]{1,0:T(8,128)(2,1)}, u32[]{:S(2)}) copy-start(bf16[288,1152]{1,0:T(8,128)(2,1)} %param.10) | copy-start | bytes 1990660
  593.7 18.5 %copy-start.13 = (bf16[4,72,1024]{2,1,0:T(8,128)(2,1)S(1)}, bf16[4,72,1024]{2,1,0:T(8,128)(2,1)}, u32[]{:S(2)}) copy-start(bf16[4,72,1024]{2,1,0:T(8,128)(2,1)} %copy-done.12) | copy-start | bytes 1769476
  593.7 223.8 %reduce-scatter.15.cloned.1.call-start = ((), (), s32[]{:S(2)}) async-start(), calls=%async_computation.13 | async-start | bytes 995328 | tf_op jit(solution)/shard_map/reduce_scatter | solution.py:176
  631.5 22.7 %copy-start.19 = (bf16[1,1024,288]{1,2,0:T(8,128)(2,1)S(1)}, bf16[1,1024,288]{1,2,0:T(8,128)(2,1)}, u32[]{:S(2)}) copy-start(bf16[1,1024,288]{1,2,0:T(8,128)(2,1)} %copy-done.18) | copy-start | bytes 1769476
  631.5 230.7 %reduce-scatter.19.cloned.1.call-start = ((), (), s32[]{:S(2)}) async-start(), calls=%async_computation.18 | async-start | bytes 2322432
  654.2 24.5 %copy-start.24 = (f32[1024]{0:T(1024)S(1)}, f32[1024]{0:T(1024)}, u32[]{:S(2)}) copy-start(f32[1024]{0:T(1024)} %copy-done.23) | copy-start | bytes 12292
  654.3 24.4 %copy-start.26 = (f32[1024]{0:T(1024)S(1)}, f32[1024]{0:T(1024)}, u32[]{:S(2)}) copy-start(f32[1024]{0:T(1024)} %copy-done.25) | copy-start | bytes 12292
  695.8 340.5 %all-reduce.5.cloned.1.call-start = ((), (), s32[]{:S(2)}) async-start(), calls=%async_computation.12 | async-start | bytes 9437184 | tf_op jit(solution)/shard_map/psum | solution.py:103
  702.1 76.8 %copy-start.6 = (bf16[1,1024,288]{1,2,0:T(8,128)(2,1)S(1)}, bf16[1,1024,288]{1,2,0:T(8,128)(2,1)}, u32[]{:S(2)}) copy-start(bf16[1,1024,288]{1,2,0:T(8,128)(2,1)} %copy.167) | copy-start | bytes 1769476
  (21 other events, 94.9 us)
Sparse Core Ops, SparseCore 0:
  9.6 53.1 all-gather.9
  97.9 84.0 reduce-scatter.10
  184.2 50.9 all-gather.7
  237.2 49.2 all-gather.11
  353.9 170.7 all-reduce.2
  561.8 47.6 all-gather.13
  612.7 33.9 reduce-scatter.16
  650.4 40.8 reduce-scatter.20
  693.6 85.2 reduce-scatter.12
  781.9 35.5 reduce-scatter.14
  821.3 40.8 reduce-scatter.18
  864.4 171.9 all-reduce.4
where the time goes:
time: 1060 us; the launch traced here: 1050 us
  waiting for transfers between devices  699 us (66%)
  matrix products  156 us (15%)
  local copies, waits for them, and re-layouts  109 us (10%)
  other arithmetic  43.7 us (4%)
  blocking collectives  28 us (3%)
  between operations  15 us (1%)
    psum x2, waiting for transfers between devices, layer_backward(): whole_sum = lax.psum(partial_term, 'heads')  342 us
    reduce_scatter x2, waiting for transfers between devices, layer_forward(): summed = lax.psum_scatter(update, 'heads', scatter_dimension=1, tiled=True)  153 us
    all_gather x4, waiting for transfers between devices, row_features(): return lax.all_gather(share_rows, 'heads', axis=1, tiled=True)  124 us
    unnamed x90, local copies, waits for them, and re-layouts  59.2 us
    unnamed x14, waiting for transfers between devices  43.9 us
    reduce_scatter x1, waiting for transfers between devices, shards(): lax.psum_scatter(spatial_out_grad.astype(jnp.bfloat16), 'seq', scatter_di...  36.5 us
    dot_general x2, matrix products, attend_backward(): jnp.einsum('bhlm,lbhd->mbhd', score_gradient, query_rows, preferred_eleme...  30.5 us
    dot_general x2, matrix products, attend_backward(): jnp.einsum('bhlm,mbhd->lbhd', score_gradient, key_matrix, preferred_eleme...  29 us
  transfers between devices with their start and end apart: 12, of which 10 were waited for; matrix products, arithmetic and copies ran while one was open for 17% of the time, Pallas kernels for 0%

commit v1 on v0

--- a/solution.py
+++ b/solution.py
@@ -16,9 +16,10 @@
 
 def normalize(full_rows):
     values = full_rows.astype(jnp.float32)
-    center = values - jnp.mean(values, axis=-1, keepdims=True)
+    mean = jnp.mean(values, axis=-1, keepdims=True)
+    center = values - mean
     inverse = lax.rsqrt(jnp.mean(center * center, axis=-1, keepdims=True) + 1e-06)
-    return (center * inverse, inverse)
+    return (center * inverse, mean, inverse)
 
 
 def attention_probs(query_rows, key_matrix, allowed):
@@ -65,10 +66,9 @@
     return (query_gradient, key_gradient, value_gradient)
 
 
-def layer_forward(share_rows, qkv_weights, out_weights, allowed, length, batch_count):
+def layer_forward(share_rows, full_rows, qkv_weights, out_weights, allowed, length, batch_count):
     own_width = share_rows.shape[1]
-    full_rows = row_features(share_rows)
-    normed, inverse = normalize(full_rows)
+    normed, mean, inverse = normalize(full_rows)
     normed_low = normed.astype(jnp.bfloat16)
     projected = jnp.einsum(
         "nd,kde->kne", normed_low, qkv_weights, preferred_element_type=jnp.float32
@@ -78,16 +78,19 @@
         length * batch_count, own_width
     )
     update = jnp.dot(blended_rows, out_weights, preferred_element_type=jnp.float32)
+    return (update.astype(jnp.bfloat16), (normed, mean, inverse, normed_low, shaped, blended_rows))
+
+
+def add_update(share_rows, update):
     summed = lax.psum_scatter(update, "heads", scatter_dimension=1, tiled=True)
-    output = (share_rows.astype(jnp.float32) + summed).astype(jnp.bfloat16)
-    return (output, (normed, inverse, normed_low, shaped, blended_rows))
-
-
-def layer_backward(grad_share, qkv_weights, out_weights, allowed, saved_state):
-    normed, inverse, normed_low, shaped, blended_rows = saved_state
-    own_width = grad_share.shape[1]
-    grad_rows = row_features(grad_share)
-    out_grad = jnp.einsum("nk,nd->kd", blended_rows, grad_rows, preferred_element_type=jnp.float32)
+    return (share_rows.astype(jnp.float32) + summed.astype(jnp.float32)).astype(jnp.bfloat16)
+
+
+def layer_backward(share_rows, grad_share, grad_rows, qkv_weights, out_weights, allowed, saved):
+    normed, mean, inverse, normed_low, shaped, blended_rows = saved
+    rows, own_width = grad_share.shape
+    groups = lax.axis_size("heads")
+    out_grad = jnp.einsum("nd,nk->dk", grad_rows, blended_rows, preferred_element_type=jnp.float32)
     grad_mixed = jnp.einsum(
         "nd,kd->nk", grad_rows, out_weights, preferred_element_type=jnp.float32
     ).astype(jnp.bfloat16)
@@ -96,19 +99,38 @@
         shaped[0], shaped[1], shaped[2], allowed, grad_mixed
     )
     qkv_grads = jnp.stack([query_gradient, key_gradient, value_gradient]).reshape(3, -1, own_width)
-    qkv_grad = jnp.einsum("nd,kne->kde", normed_low, qkv_grads, preferred_element_type=jnp.float32)
+    qkv_grad = jnp.einsum("nd,kne->dke", normed_low, qkv_grads, preferred_element_type=jnp.float32)
+    weight_grads = jnp.concatenate([qkv_grad, out_grad[:, None]], axis=1).astype(jnp.bfloat16)
+    weight_grads = weight_grads.reshape(-1, 4 * own_width)
     partial_term = jnp.einsum(
-        "kne,kde->nd", qkv_grads, qkv_weights, preferred_element_type=jnp.float32
-    )
-    whole_sum = lax.psum(partial_term, "heads")
-    mean_first = jnp.mean(whole_sum, axis=-1, keepdims=True)
-    mean_second = jnp.mean(whole_sum * normed, axis=-1, keepdims=True)
-    full_grad = inverse * (whole_sum - mean_first - normed * mean_second)
-    own_grad = lax.dynamic_slice_in_dim(
-        full_grad, lax.axis_index("heads") * own_width, own_width, 1
-    )
+        "kne,kde->dn", qkv_grads, qkv_weights, preferred_element_type=jnp.float32
+    )
+    features = partial_term.shape[0]
+    first = jnp.sum(partial_term, axis=0) / features
+    second = jnp.sum(partial_term * normed.T, axis=0) / features
+    extra = jnp.concatenate([first[None], second[None], jnp.zeros((14, rows), jnp.float32)])
+    packed = jnp.concatenate(
+        [
+            partial_term.reshape(groups, own_width, rows).astype(jnp.bfloat16),
+            jnp.broadcast_to(extra.astype(jnp.bfloat16)[None], (groups, 16, rows)),
+        ],
+        axis=1,
+    ).reshape(groups * (own_width + 16), rows)
+    summed = lax.psum_scatter(packed, "heads", scatter_dimension=0, tiled=True)
+    summed = summed.astype(jnp.float32)
+    whole = summed[:own_width].T
+    mean_first = summed[own_width][:, None]
+    mean_second = summed[own_width + 1][:, None]
+    own_normed = (share_rows.astype(jnp.float32) - mean) * inverse
+    own_grad = inverse * (whole - mean_first - own_normed * mean_second)
     grad_in = (grad_share.astype(jnp.float32) + own_grad).astype(jnp.bfloat16)
-    return (grad_in, qkv_grad, out_grad)
+    return (grad_in, weight_grads)
+
+
+def sum_weight_grads(weight_grads, own_width):
+    summed = lax.psum_scatter(weight_grads, "seq", scatter_dimension=0, tiled=True)
+    summed = summed.astype(jnp.float32).reshape(-1, 4, own_width)
+    return (jnp.swapaxes(summed[:, :3], 0, 1), summed[:, 3].T)
 
 
 def shards(
@@ -142,46 +164,50 @@
     causal = (frame_ids[:, None] >= frame_ids[None, :])[None]
     diagonal = (frame_ids[:, None] == frame_ids[None, :])[None]
     temporal_allowed = causal & ((picked == 1) | diagonal)
-    hidden, spatial_state = layer_forward(
-        frames.reshape(length, own_width), qkv_spatial, out_spatial, spatial_allowed, length, 1
-    )
-    by_position = relayout(hidden.reshape(1, length, own_width))
-    result, temporal_state = layer_forward(
-        by_position.reshape(length, own_width),
+    frame_share = frames.reshape(length, own_width)
+    cotangent_share = cotangent.reshape(length, own_width)
+    frame_rows = row_features(frame_share)
+    cotangent_share, frame_rows = lax.optimization_barrier((cotangent_share, frame_rows))
+    cotangent_rows = row_features(cotangent_share)
+    update, spatial_state = layer_forward(
+        frame_share, frame_rows, qkv_spatial, out_spatial, spatial_allowed, length, 1
+    )
+    hidden = add_update(frame_share, update)
+    position_share = relayout(hidden.reshape(1, length, own_width)).reshape(length, own_width)
+    position_rows = row_features(position_share)
+    late_update, temporal_state = layer_forward(
+        position_share,
+        position_rows,
         qkv_temporal,
         out_temporal,
         temporal_allowed,
         frame_count,
         local_count,
     )
-    grad_position, temporal_qkv_grad, temporal_out_grad = layer_backward(
-        cotangent.reshape(length, own_width),
+    grad_position, temporal_grads = layer_backward(
+        position_share,
+        cotangent_share,
+        cotangent_rows,
         qkv_temporal,
         out_temporal,
         temporal_allowed,
         temporal_state,
     )
-    hidden_grad = relayout(grad_position.reshape(1, length, own_width))
-    frames_grad, spatial_qkv_grad, spatial_out_grad = layer_backward(
-        hidden_grad.reshape(length, own_width),
+    hidden_grad = relayout(grad_position.reshape(1, length, own_width)).reshape(length, own_width)
+    hidden_grad_rows = row_features(hidden_grad)
+    late_update, hidden_grad_rows = lax.optimization_barrier((late_update, hidden_grad_rows))
+    result = add_update(position_share, late_update)
+    frames_grad, spatial_grads = layer_backward(
+        frame_share,
+        hidden_grad,
+        hidden_grad_rows,
         qkv_spatial,
         out_spatial,
         spatial_allowed,
         spatial_state,
     )
-    reduced = (
-        lax.psum_scatter(
-            spatial_qkv_grad.astype(jnp.bfloat16), "seq", scatter_dimension=1, tiled=True
-        ).astype(jnp.float32),
-        lax.psum_scatter(
-            spatial_out_grad.astype(jnp.bfloat16), "seq", scatter_dimension=1, tiled=True
-        ).astype(jnp.float32),
-        lax.psum_scatter(
-            temporal_qkv_grad.astype(jnp.bfloat16), "seq", scatter_dimension=1, tiled=True
-        ).astype(jnp.float32),
-        lax.psum_scatter(
-            temporal_out_grad.astype(jnp.bfloat16), "seq", scatter_dimension=1, tiled=True
-        ).astype(jnp.float32),
+    reduced = sum_weight_grads(spatial_grads, own_width) + sum_weight_grads(
+        temporal_grads, own_width
     )
     return (
         result.reshape(frame_count, local_count, own_width),

time: 1060 us -> 708 us (0.67)
  waiting for transfers between devices: 699 us -> 353 us
    psum x2 -> x0, waiting for transfers between devices: 342 us -> none  [layer_backward(): whole_sum = lax.psum(partial_term, 'heads')]
    unnamed x90 -> x87, local copies, waits for them, and re-layouts: 59.2 us -> 25.5 us
    reduce_scatter x4 -> x5, waiting for transfers between devices: 190 us -> 163 us  [the longest x2 98.7 us: layer_backward(): summed = lax.psum_scatter(packed, 'heads', scatter_dimension=0, tiled=True)]
    convert_element_type x0 -> x6, local copies, waits for them, and re-layouts: none -> 22.4 us  [the longest x4 11.9 us: layer_backward(): partial_term.reshape(groups, own_width, rows).astype(jnp.bfloat16)]
    all_gather x4, waiting for transfers between devices: 124 us -> 141 us  [row_features(): return lax.all_gather(share_rows, 'heads', axis=1, tiled=True)]
    unnamed x14 -> x11, waiting for transfers between devices: 43.9 us -> 48.3 us
  transfers between devices with their start and end apart: 12 -> 10, of which waited for: 10 -> 9; matrix products, arithmetic and copies ran while one was open for 17% -> 23% of each run, Pallas kernels for 0% -> 0%
where the time goes in v1:
time: 708 us; the launch traced here: 698 us
  waiting for transfers between devices  353 us (50%)
  matrix products  148 us (21%)
  local copies, waits for them, and re-layouts  112 us (16%)
  other arithmetic  39.9 us (6%)
  blocking collectives  28 us (4%)
  between operations  15.3 us (2%)
    all_gather x4, waiting for transfers between devices, row_features(): return lax.all_gather(share_rows, 'heads', axis=1, tiled=True)  141 us
    reduce_scatter x2, waiting for transfers between devices, layer_backward(): summed = lax.psum_scatter(packed, 'heads', scatter_dimension=0, tiled=True)  98.7 us
    unnamed x11, waiting for transfers between devices  48.3 us
    reduce_scatter x1, waiting for transfers between devices, add_update(): summed = lax.psum_scatter(update, 'heads', scatter_dimension=1, tiled=True)  46.1 us
    dot_general x2, matrix products, attend_backward(): jnp.einsum('bhlm,lbhd->mbhd', score_gradient, query_rows, preferred_eleme...  29.4 us
    dot_general x2, matrix products, attend_backward(): jnp.einsum('bhlm,mbhd->lbhd', score_gradient, key_matrix, preferred_eleme...  29.2 us
    all_to_all x2, blocking collectives, relayout(): lax.all_to_all(block_rows, 'seq', split_axis=1, concat_axis=0, tiled=True)  28 us
    unnamed x87, local copies, waits for them, and re-layouts  25.5 us
  transfers between devices with their start and end apart: 10, of which 9 were waited for; matrix products, arithmetic and copies ran while one was open for 23% of the time, Pallas kernels for 0%

profile of v1, /device:TPU:0, one launch (start us, length us, event | category | flops | bytes accessed | tf_op | source)
XLA Modules:
  0.0 697.6 jit_solution(15220643222863065959)
XLA Ops:
  13.0 49.8 %all-gather.10.cloned.1.call-done = bf16[1,1024,1152]{1,2,0:T(8,128)(2,1)} async-done(((bf16[1,1024,288]{1,2,0:T(8,128)(2,1)}), bf16[1,1024,1152]{1,2,0:T(8,128)(2,1)}) %all-gather.10.cloned.1.call-update) | async-done | bytes 2359312 | tf_op jit(solution)/shard_map/all_gather | solution.py:10
  74.1 11.9 %fusion.123 = (f32[4,1024]{1,0:T(4,128)S(1)}, f32[4,1024,1024]{1,2,0:T(8,128)}) fusion(pred[1024,1024]{0,1:T(8,128)(4,1)} %bitcast_or_fusion, bf16[1024,4,72]{0,2,1:T(8,128)(2,1)S(1)} %bitcast.276, bf16[1024,4,72]{0,2,1:T(8,128)(2,1)} %bitcast.278), kind=kOutput, calls=%fused_computation.177 | convolution fusion | flops 620758016 | bytes 19021824 | tf_op jit(solution)/shard_map/sub | solution.py:30
  86.0 7.5 %fusion.56 = bf16[4,72,1024]{2,1,0:T(8,128)(2,1)S(1)} fusion(bf16[1024,4,72]{0,2,1:T(8,128)(2,1)S(1)} %bitcast.266, f32[4,1024,1024]{1,2,0:T(8,128)} %get-tuple-element.71, f32[4,1024]{1,0:T(4,128)S(1)} %get-tuple-element.70), kind=kOutput, calls=%fused_computation.82 | convolution fusion | flops 612663296 | bytes 17973248 | tf_op jit(solution)/shard_map/bhlm,mbhd->lbhd/dot_general | solution.py:36
  98.1 46.1 %reduce-scatter.11.cloned.1.call-done = bf16[1024,288]{0,1:T(8,128)(2,1)} async-done(((bf16[1024,1152]{0,1:T(8,128)(2,1)}), bf16[1024,288]{0,1:T(8,128)(2,1)}) %reduce-scatter.11.cloned.1.call-update) | async-done | bytes 589840 | tf_op jit(solution)/shard_map/reduce_scatter | solution.py:85
  149.1 6.6 reduce.11
  156.8 13.9 %all_to_all.8 = bf16[8,2,18432]{2,1,0:T(2,128)(2,1)S(1)} all-to-all(bf16[8,2,18432]{2,1,0:T(2,128)(2,1)S(1)} %reshape.463), channel_id=1, replica_groups=mesh['heads'=4,'seq'=8] {'seq'}, dimensions={0} | all-to-all | bytes 1179648 | tf_op jit(solution)/shard_map/all_to_all | solution.py:14
  179.7 16.6 %all-gather.8.cloned.1.call-done = bf16[1024,1152]{0,1:T(8,128)(2,1)} async-done(((bf16[1024,288]{0,1:T(8,128)(2,1)}), bf16[1024,1152]{0,1:T(8,128)(2,1)}) %all-gather.8.cloned.1.call-update) | async-done | bytes 2359312 | tf_op jit(solution)/shard_map/all_gather | solution.py:10
  201.2 46.4 %all-gather.12.cloned.1.call-done = bf16[1,1024,1152]{1,2,0:T(8,128)(2,1)} async-done(((bf16[1,1024,288]{1,2,0:T(8,128)(2,1)}), bf16[1,1024,1152]{1,2,0:T(8,128)(2,1)}) %all-gather.12.cloned.1.call-update) | async-done | bytes 2359312 | tf_op jit(solution)/shard_map/all_gather | solution.py:10
  271.7 5.3 fusion.124
  277.1 6.4 fusion.47
  283.4 6.2 fusion.48
  325.6 49.0 %reduce-scatter.19.cloned.1.call-done = bf16[304,1024]{1,0:T(8,128)(2,1)} async-done(((bf16[1216,1024]{1,0:T(8,128)(2,1)}), bf16[304,1024]{1,0:T(8,128)(2,1)}) %reduce-scatter.19.cloned.1.call-update) | async-done | bytes 622608 | tf_op jit(solution)/shard_map/reduce_scatter | solution.py:119
  380.1 6.6 reduce.12
  387.8 14.1 %all_to_all.9 = bf16[8,2,18432]{2,1,0:T(2,128)(2,1)S(1)} all-to-all(bf16[8,2,18432]{2,1,0:T(2,128)(2,1)S(1)} %reshape.465), channel_id=1, replica_groups=mesh['heads'=4,'seq'=8] {'seq'}, dimensions={0} | all-to-all | bytes 1179648 | tf_op jit(solution)/shard_map/all_to_all | solution.py:14
  421.7 5.3 copy.251
  430.2 28.4 %all-gather.14.cloned.1.call-done = bf16[1,1024,1152]{1,2,0:T(8,128)(2,1)} async-done(((bf16[1,1024,288]{1,2,0:T(8,128)(2,1)}), bf16[1,1024,1152]{1,2,0:T(8,128)(2,1)}) %all-gather.14.cloned.1.call-update) | async-done | bytes 2359312 | tf_op jit(solution)/shard_map/all_gather | solution.py:10
  465.6 8.9 %fusion.126 = f32[4,1024,1024]{1,2,0:T(8,128)} fusion(bf16[1024,4,72]{0,2,1:T(8,128)(2,1)S(1)} %bitcast.274, bf16[1024,4,72]{0,2,1:T(8,128)(2,1)S(1)} %bitcast.267), kind=kOutput, calls=%fused_computation.180 | convolution fusion | flops 603979776 | bytes 17956864 | tf_op jit(solution)/shard_map/lbhd,mbhd->bhlm/dot_general | solution.py:53
  474.5 22.8 %fusion.50 = bf16[4,72,1024]{2,1,0:T(8,128)(2,1)S(1)} fusion(bf16[1024,4,72]{0,2,1:T(8,128)(2,1)S(1)} %bitcast.279, f32[4,1024,1024]{1,2,0:T(8,128)} %fusion.126, f32[4,1024,1024]{1,2,0:T(8,128)} %get-tuple-element.71, f32[4,1024]{1,0:T(4,128)S(1)} %get-tuple-element.70), kind=kOutput, calls=%fused_computation.80 | convolution fusion | flops 633639936 | bytes 34750464 | tf_op jit(solution)/shard_map/bhlm,mbhd->lbhd/dot_general | solution.py:60
  497.3 23.2 %fusion.53 = bf16[4,72,1024]{2,1,0:T(8,128)(2,1)} fusion(bf16[1024,4,72]{0,2,1:T(8,128)(2,1)S(1)} %bitcast.277, f32[4,1024,1024]{1,2,0:T(8,128)} %fusion.126, f32[4,1024,1024]{1,2,0:T(8,128)} %get-tuple-element.71, f32[4,1024]{1,0:T(4,128)S(1)} %get-tuple-element.70), kind=kOutput, calls=%fused_computation.81 | convolution fusion | flops 633639936 | bytes 34750464 | tf_op jit(solution)/shard_map/bhlm,lbhd->mbhd/dot_general | solution.py:63
  523.2 8.6 %fusion.59 = bf16[4,72,1024]{2,1,0:T(8,128)(2,1)S(1)} fusion(bf16[1024,4,72]{0,2,1:T(8,128)(2,1)S(1)} %bitcast.275, f32[4,1024,1024]{1,2,0:T(8,128)} %get-tuple-element.71, f32[4,1024]{1,0:T(4,128)S(1)} %get-tuple-element.70), kind=kOutput, calls=%fused_computation.83 | convolution fusion | flops 612663296 | bytes 17973248 | tf_op jit(solution)/shard_map/bhlm,lbhd->mbhd/dot_general | solution.py:47
  547.2 6.2 bitcast_reduce_fusion
  566.5 18.2 %reduce-scatter.15.cloned.1.call-done = bf16[144,1152]{1,0:T(8,128)(2,1)} async-done(((bf16[1152,1152]{1,0:T(8,128)(2,1)}), bf16[144,1152]{1,0:T(8,128)(2,1)}) %reduce-scatter.15.cloned.1.call-update) | async-done | bytes 331792 | tf_op jit(solution)/shard_map/reduce_scatter | solution.py:131
  588.3 46.8 %reduce-scatter.21.cloned.1.call-done = bf16[288,1024]{1,0:T(8,128)(2,1)} async-done(((bf16[1152,1024]{1,0:T(8,128)(2,1)}), bf16[288,1024]{1,0:T(8,128)(2,1)}) %reduce-scatter.21.cloned.1.call-update) | async-done | bytes 589840
  637.2 49.8 %reduce-scatter.13.cloned.1.call-done = bf16[304,1024]{1,0:T(8,128)(2,1)} async-done(((bf16[1216,1024]{1,0:T(8,128)(2,1)}), bf16[304,1024]{1,0:T(8,128)(2,1)}) %reduce-scatter.13.cloned.1.call-update) | async-done | bytes 622608 | tf_op jit(solution)/shard_map/reduce_scatter | solution.py:119
  (199 shorter events, 177.7 us)
Async XLA Ops:
  7.2 248.0 %copy-start = (bf16[3,1152,288]{1,2,0:T(8,128)(2,1)S(1)}, bf16[3,1152,288]{1,2,0:T(8,128)(2,1)}, u32[]{:S(2)}) copy-start(bf16[3,1152,288]{1,2,0:T(8,128)(2,1)} %param.11) | copy-start | bytes 5971972
  7.2 55.6 %all-gather.10.cloned.1.call-start = ((), (), s32[]{:S(2)}) async-start(), calls=%async_computation.13 | async-start | bytes 2949120 | tf_op jit(solution)/shard_map/all_gather | solution.py:10
  7.9 136.3 %reduce-scatter.11.cloned.1.call-start = ((), (), s32[]{:S(2)}) async-start(), calls=%async_computation.8 | async-start | bytes 2949120 | tf_op jit(solution)/shard_map/reduce_scatter | solution.py:85
  74.1 11.9 %copy-start.14 = (bf16[1,1024,288]{1,2,0:T(8,128)(2,1)}, bf16[1,1024,288]{1,2,0:T(8,128)(2,1)S(1)}, u32[]{:S(2)}) copy-start(bf16[1,1024,288]{1,2,0:T(8,128)(2,1)S(1)} %get-tuple-element.64) | copy-start | bytes 1769476
  74.1 11.9 %copy-start.12 = (bf16[1,1024,288]{1,2,0:T(8,128)(2,1)}, bf16[1,1024,288]{1,2,0:T(8,128)(2,1)S(1)}, u32[]{:S(2)}) copy-start(bf16[1,1024,288]{1,2,0:T(8,128)(2,1)S(1)} %get-tuple-element.65) | copy-start | bytes 1769476
  97.1 47.0 %copy-start.8 = (bf16[1,1024,288]{1,2,0:T(8,128)(2,1)S(1)}, bf16[1,1024,288]{1,2,0:T(8,128)(2,1)}, u32[]{:S(2)}) copy-start(bf16[1,1024,288]{1,2,0:T(8,128)(2,1)} %param.8) | copy-start | bytes 1769476
  97.2 99.2 %all-gather.8.cloned.1.call-start = ((), (), s32[]{:S(2)}) async-start(), calls=%async_computation.9 | async-start | bytes 2949120 | tf_op jit(solution)/shard_map/all_gather | solution.py:10
  97.9 149.8 %all-gather.12.cloned.1.call-start = ((), (), s32[]{:S(2)}) async-start(), calls=%async_computation.14 | async-start | bytes 2949120 | tf_op jit(solution)/shard_map/all_gather | solution.py:10
  179.0 195.6 %reduce-scatter.19.cloned.1.call-start = ((), (), s32[]{:S(2)}) async-start(), calls=%async_computation.16 | async-start | bytes 3112960 | tf_op jit(solution)/shard_map/reduce_scatter | solution.py:119
  325.5 51.1 %copy-start.7 = (bf16[1,1024,288]{1,2,0:T(8,128)(2,1)S(1)}, bf16[1,1024,288]{1,2,0:T(8,128)(2,1)}, u32[]{:S(2)}) copy-start(bf16[1,1024,288]{1,2,0:T(8,128)(2,1)} %copy.220) | copy-start | bytes 1769476
  325.5 51.1 %copy-start.10 = (bf16[1024,288]{0,1:T(8,128)(2,1)S(1)}, bf16[1024,288]{0,1:T(8,128)(2,1)}, u32[]{:S(2)}) copy-start(bf16[1024,288]{0,1:T(8,128)(2,1)} %copy_bitcast_fusion) | copy-start | bytes 1769476
  325.5 133.1 %all-gather.14.cloned.1.call-start = ((), (), s32[]{:S(2)}) async-start(), calls=%async_computation.15 | async-start | bytes 2949120 | tf_op jit(solution)/shard_map/all_gather | solution.py:10
  410.2 152.8 %reduce-scatter.17.cloned.1.call-start = ((), (), s32[]{:S(2)}) async-start(), calls=%async_computation.12 | async-start | bytes 2985984 | tf_op jit(solution)/shard_map/reduce_scatter | solution.py:131
  429.9 33.0 %copy-start.27 = (bf16[288,1152]{1,0:T(8,128)(2,1)S(1)}, bf16[288,1152]{1,0:T(8,128)(2,1)}, u32[]{:S(2)}) copy-start(bf16[288,1152]{1,0:T(8,128)(2,1)} %param.10) | copy-start | bytes 1990660
  429.9 154.8 %reduce-scatter.15.cloned.1.call-start = ((), (), s32[]{:S(2)}) async-start(), calls=%async_computation.11 | async-start | bytes 2985984 | tf_op jit(solution)/shard_map/reduce_scatter | solution.py:131
  465.6 8.9 %copy-start.16 = (bf16[1,1024,288]{1,2,0:T(8,128)(2,1)S(1)}, bf16[1,1024,288]{1,2,0:T(8,128)(2,1)}, u32[]{:S(2)}) copy-start(bf16[1,1024,288]{1,2,0:T(8,128)(2,1)} %get-tuple-element.63) | copy-start | bytes 1769476
  474.5 22.8 %copy-start.15 = (bf16[1,1024,288]{1,2,0:T(8,128)(2,1)S(1)}, bf16[1,1024,288]{1,2,0:T(8,128)(2,1)}, u32[]{:S(2)}) copy-start(bf16[1,1024,288]{1,2,0:T(8,128)(2,1)} %copy-done.14) | copy-start | bytes 1769476
  497.3 23.2 %copy-start.29 = (bf16[4,72,1024]{2,1,0:T(8,128)(2,1)S(1)}, bf16[4,72,1024]{2,1,0:T(8,128)(2,1)}, u32[]{:S(2)}) copy-start(bf16[4,72,1024]{2,1,0:T(8,128)(2,1)} %copy-done.28) | copy-start | bytes 1769476
  523.1 8.6 %copy-start.3 = (bf16[1,1024,1152]{2,1,0:T(8,128)(2,1)S(1)}, bf16[1,1024,1152]{2,1,0:T(8,128)(2,1)}, u32[]{:S(2)}) copy-start(bf16[1,1024,1152]{2,1,0:T(8,128)(2,1)} %copy.216) | copy-start | bytes 7077892
  523.1 8.6 %copy-start.20 = (f32[1024]{0:T(1024)S(1)}, f32[1024]{0:T(1024)}, u32[]{:S(2)}) copy-start(f32[1024]{0:T(1024)} %copy-done.19) | copy-start | bytes 12292
  541.6 93.6 %reduce-scatter.21.cloned.1.call-start = ((), (), s32[]{:S(2)}) async-start(), calls=%async_computation.17 | async-start | bytes 2949120
  546.2 140.8 %reduce-scatter.13.cloned.1.call-start = ((), (), s32[]{:S(2)}) async-start(), calls=%async_computation.10 | async-start | bytes 3112960 | tf_op jit(solution)/shard_map/reduce_scatter | solution.py:119
  587.6 101.4 %copy-start.9 = (bf16[1,1024,288]{1,2,0:T(8,128)(2,1)S(1)}, bf16[1,1024,288]{1,2,0:T(8,128)(2,1)}, u32[]{:S(2)}) copy-start(bf16[1,1024,288]{1,2,0:T(8,128)(2,1)} %param.8) | copy-start | bytes 1769476
  587.6 101.4 %copy-start.11 = (bf16[1,1024,288]{1,2,0:T(8,128)(2,1)S(1)}, bf16[1,1024,288]{1,2,0:T(8,128)(2,1)}, u32[]{:S(2)}) copy-start(bf16[1,1024,288]{1,2,0:T(8,128)(2,1)} %copy.242) | copy-start | bytes 1769476
  (21 other events, 92.9 us)
Sparse Core Ops, SparseCore 0:
  9.6 53.1 all-gather.9
  97.3 46.8 reduce-scatter.10
  146.3 49.9 all-gather.7
  198.3 49.2 all-gather.11
  325.7 48.8 reduce-scatter.18
  410.3 48.2 all-gather.13
  462.1 42.5 reduce-scatter.16
  541.7 43.0 reduce-scatter.14
  587.1 48.0 reduce-scatter.20
  637.3 49.5 reduce-scatter.12

commit v2 on v1

--- a/solution.py
+++ b/solution.py
@@ -86,7 +86,9 @@
     return (share_rows.astype(jnp.float32) + summed.astype(jnp.float32)).astype(jnp.bfloat16)
 
 
-def layer_backward(share_rows, grad_share, grad_rows, qkv_weights, out_weights, allowed, saved):
+def layer_backward(
+    share_rows, grad_share, grad_rows, qkv_weights, out_weights, allowed, saved, before=()
+):
     normed, mean, inverse, normed_low, shaped, blended_rows = saved
     rows, own_width = grad_share.shape
     groups = lax.axis_size("heads")
@@ -116,6 +118,7 @@
         ],
         axis=1,
     ).reshape(groups * (own_width + 16), rows)
+    packed, before = lax.optimization_barrier((packed, before))
     summed = lax.psum_scatter(packed, "heads", scatter_dimension=0, tiled=True)
     summed = summed.astype(jnp.float32)
     whole = summed[:own_width].T
@@ -124,12 +127,18 @@
     own_normed = (share_rows.astype(jnp.float32) - mean) * inverse
     own_grad = inverse * (whole - mean_first - own_normed * mean_second)
     grad_in = (grad_share.astype(jnp.float32) + own_grad).astype(jnp.bfloat16)
-    return (grad_in, weight_grads)
-
-
-def sum_weight_grads(weight_grads, own_width):
-    summed = lax.psum_scatter(weight_grads, "seq", scatter_dimension=0, tiled=True)
-    summed = summed.astype(jnp.float32).reshape(-1, 4, own_width)
+    return (grad_in, weight_grads, before)
+
+
+def exchange_grads(weight_grads):
+    members = lax.axis_size("seq")
+    blocks = weight_grads.reshape(members, -1, weight_grads.shape[1])
+    shares = lax.all_to_all(blocks, "seq", split_axis=0, concat_axis=0, tiled=True)
+    return jnp.sum(shares.astype(jnp.float32), axis=0)
+
+
+def split_grads(summed, own_width):
+    summed = summed.reshape(-1, 4, own_width)
     return (jnp.swapaxes(summed[:, :3], 0, 1), summed[:, 3].T)
 
 
@@ -168,11 +177,16 @@
     cotangent_share = cotangent.reshape(length, own_width)
     frame_rows = row_features(frame_share)
     cotangent_share, frame_rows = lax.optimization_barrier((cotangent_share, frame_rows))
-    cotangent_rows = row_features(cotangent_share)
+    half = length // 2
+    early_rows = row_features(cotangent_share[:half])
     update, spatial_state = layer_forward(
         frame_share, frame_rows, qkv_spatial, out_spatial, spatial_allowed, length, 1
     )
+    update, early_rows = lax.optimization_barrier((update, early_rows))
     hidden = add_update(frame_share, update)
+    late_cotangent, hidden = lax.optimization_barrier((cotangent_share[half:], hidden))
+    late_rows = row_features(late_cotangent)
+    cotangent_rows = jnp.concatenate([early_rows, late_rows])
     position_share = relayout(hidden.reshape(1, length, own_width)).reshape(length, own_width)
     position_rows = row_features(position_share)
     late_update, temporal_state = layer_forward(
@@ -184,7 +198,7 @@
         frame_count,
         local_count,
     )
-    grad_position, temporal_grads = layer_backward(
+    grad_position, temporal_grads, _ = layer_backward(
         position_share,
         cotangent_share,
         cotangent_rows,
@@ -195,9 +209,12 @@
     )
     hidden_grad = relayout(grad_position.reshape(1, length, own_width)).reshape(length, own_width)
     hidden_grad_rows = row_features(hidden_grad)
-    late_update, hidden_grad_rows = lax.optimization_barrier((late_update, hidden_grad_rows))
+    late_update, temporal_grads, hidden_grad_rows = lax.optimization_barrier(
+        (late_update, temporal_grads, hidden_grad_rows)
+    )
     result = add_update(position_share, late_update)
-    frames_grad, spatial_grads = layer_backward(
+    temporal_sums = lax.psum_scatter(temporal_grads, "seq", scatter_dimension=0, tiled=True)
+    frames_grad, spatial_grads, early = layer_backward(
         frame_share,
         hidden_grad,
         hidden_grad_rows,
@@ -205,9 +222,11 @@
         out_spatial,
         spatial_allowed,
         spatial_state,
-    )
-    reduced = sum_weight_grads(spatial_grads, own_width) + sum_weight_grads(
-        temporal_grads, own_width
+        (result, temporal_sums),
+    )
+    result, temporal_sums = early
+    reduced = split_grads(exchange_grads(spatial_grads), own_width) + split_grads(
+        temporal_sums.astype(jnp.float32), own_width
     )
     return (
         result.reshape(frame_count, local_count, own_width),

time: 708 us -> 645 us (0.911)
  waiting for transfers between devices: 353 us -> 234 us
  blocking collectives: 28 us -> 64.3 us
  local copies, waits for them, and re-layouts: 112 us -> 130 us
    reduce_scatter x2 -> x1, waiting for transfers between devices: 98.7 us -> 49 us  [layer_backward(): summed = lax.psum_scatter(packed, 'heads', scatter_dimension=0, tiled=True)]
    reduce_scatter x3 -> x1, waiting for transfers between devices: 64.3 us -> 18.5 us  [shards(): lax.psum_scatter(temporal_grads, 'seq', scatter_dimension=0, tiled=True)]
    all_to_all x0 -> x1, blocking collectives: none -> 36.3 us  [exchange_grads(): lax.all_to_all(blocks, 'seq', split_axis=0, concat_axis=0, tiled=True)]
    all_gather x4 -> x5, waiting for transfers between devices: 141 us -> 120 us  [row_features(): return lax.all_gather(share_rows, 'heads', axis=1, tiled=True)]
    unnamed x87 -> x100, local copies, waits for them, and re-layouts: 25.5 us -> 39.8 us
    concatenate x0 -> x2, local copies, waits for them, and re-layouts: none -> 9.88 us  [the longest x1 7.35 us: layer_backward(): jnp.concatenate([qkv_grad, out_grad[:, None]], axis=1).astype(jnp.bfloat16)]
    unnamed x3 -> x2, other arithmetic: 15.2 us -> 12.1 us
    unnamed x11 -> x13, waiting for transfers between devices: 48.3 us -> 46.5 us
  transfers between devices with their start and end apart: 10 -> 10, of which waited for: 9 -> 7; matrix products, arithmetic and copies ran while one was open for 23% -> 31% of each run, Pallas kernels for 0% -> 0%
where the time goes in v2:
time: 645 us; the launch traced here: 634 us
  waiting for transfers between devices  234 us (36%)
  matrix products  148 us (23%)
  local copies, waits for them, and re-layouts  130 us (20%)
  blocking collectives  64.3 us (10%)
  other arithmetic  41.4 us (6%)
  between operations  15.2 us (2%)
    all_gather x5, waiting for transfers between devices, row_features(): return lax.all_gather(share_rows, 'heads', axis=1, tiled=True)  120 us
    reduce_scatter x1, waiting for transfers between devices, layer_backward(): summed = lax.psum_scatter(packed, 'heads', scatter_dimension=0, tiled=True)  49 us
    unnamed x13, waiting for transfers between devices  46.5 us
    unnamed x100, local copies, waits for them, and re-layouts  39.8 us
    all_to_all x1, blocking collectives, exchange_grads(): lax.all_to_all(blocks, 'seq', split_axis=0, concat_axis=0, tiled=True)  36.3 us
    dot_general x2, matrix products, attend_backward(): jnp.einsum('bhlm,mbhd->lbhd', score_gradient, key_matrix, preferred_eleme...  29.4 us
    dot_general x2, matrix products, attend_backward(): jnp.einsum('bhlm,lbhd->mbhd', score_gradient, query_rows, preferred_eleme...  28.5 us
    all_to_all x2, blocking collectives, relayout(): lax.all_to_all(block_rows, 'seq', split_axis=1, concat_axis=0, tiled=True)  28 us
  transfers between devices with their start and end apart: 10, of which 7 were waited for; matrix products, arithmetic and copies ran while one was open for 31% of the time, Pallas kernels for 0%

profile of v2, /device:TPU:0, one launch (start us, length us, event | category | flops | bytes accessed | tf_op | source)
XLA Modules:
  0.0 634.3 jit_solution(2972741260753944677)
XLA Ops:
  12.2 50.6 %all-gather.13.cloned.1.call-done = bf16[1,1024,1152]{1,2,0:T(8,128)(2,1)} async-done(((bf16[1,1024,288]{1,2,0:T(8,128)(2,1)}), bf16[1,1024,1152]{1,2,0:T(8,128)(2,1)}) %all-gather.13.cloned.1.call-update) | async-done | bytes 2359312 | tf_op jit(solution)/shard_map/all_gather | solution.py:10
  71.3 4.9 convert_bitcast_fusion.2
  77.3 11.9 %fusion.121 = (f32[4,1024]{1,0:T(4,128)S(1)}, f32[4,1024,1024]{1,2,0:T(8,128)}) fusion(pred[1024,1024]{0,1:T(8,128)(4,1)} %bitcast_or_fusion, bf16[1024,4,72]{0,2,1:T(8,128)(2,1)} %bitcast.275, bf16[1024,4,72]{0,2,1:T(8,128)(2,1)} %bitcast.277), kind=kOutput, calls=%fused_computation.180 | convolution fusion | flops 620758016 | bytes 19021824 | tf_op jit(solution)/shard_map/sub | solution.py:30
  89.2 7.5 %fusion.64 = bf16[4,72,1024]{2,1,0:T(8,128)(2,1)S(1)} fusion(bf16[1024,4,72]{0,2,1:T(8,128)(2,1)S(1)} %bitcast.266, f32[4,1024,1024]{1,2,0:T(8,128)} %get-tuple-element.71, f32[4,1024]{1,0:T(4,128)S(1)} %get-tuple-element.70), kind=kOutput, calls=%fused_computation.92 | convolution fusion | flops 612663296 | bytes 17973248 | tf_op jit(solution)/shard_map/bhlm,mbhd->lbhd/dot_general | solution.py:36
  106.6 45.6 %reduce-scatter.16.cloned.1.call-done = bf16[288,1024]{1,0:T(8,128)(2,1)} async-done(((bf16[1152,1024]{1,0:T(8,128)(2,1)}), bf16[288,1024]{1,0:T(8,128)(2,1)}) %reduce-scatter.16.cloned.1.call-update) | async-done | bytes 589840
  160.8 6.5 %reduce.15 = bf16[1024,288]{1,0:T(8,128)(2,1)S(1)} reduce(bf16[1024,1,288]{2,1,0:T(2,128)(2,1)} %bitcast.262, bf16[]{:T(256)} %broadcast.334), dimensions={1}, to_apply=%bitcast.247.reduce_sub_computation | reduce | bytes 1179650
  169.2 14.1 %all_to_all.23 = bf16[8,2,18432]{2,1,0:T(2,128)(2,1)S(1)} all-to-all(bf16[8,2,18432]{2,1,0:T(2,128)(2,1)} %reshape.462), channel_id=1, replica_groups=mesh['heads'=4,'seq'=8] {'seq'}, dimensions={0} | all-to-all | bytes 1179648 | tf_op jit(solution)/shard_map/all_to_all | solution.py:14
  186.9 4.6 copy.113
  202.5 37.3 %all-gather.15.cloned.1.call-done = bf16[1,1024,1152]{1,2,0:T(8,128)(2,1)} async-done(((bf16[1,1024,288]{1,2,0:T(8,128)(2,1)}), bf16[1,1024,1152]{1,2,0:T(8,128)(2,1)}) %all-gather.15.cloned.1.call-update) | async-done | bytes 2359312 | tf_op jit(solution)/shard_map/all_gather | solution.py:10
  275.3 6.2 fusion.55
  281.5 6.1 fusion.56
  316.4 49.0 %reduce-scatter.18.cloned.1.call-done = bf16[304,1024]{1,0:T(8,128)(2,1)} async-done(((bf16[1216,1024]{1,0:T(8,128)(2,1)}), bf16[304,1024]{1,0:T(8,128)(2,1)}) %reduce-scatter.18.cloned.1.call-update) | async-done | bytes 622608 | tf_op jit(solution)/shard_map/reduce_scatter | solution.py:122
  372.6 5.6 reduce.16
  379.4 13.9 %all_to_all.24 = bf16[8,2,18432]{2,1,0:T(2,128)(2,1)S(1)} all-to-all(bf16[8,2,18432]{2,1,0:T(2,128)(2,1)S(1)} %reshape.464), channel_id=1, replica_groups=mesh['heads'=4,'seq'=8] {'seq'}, dimensions={0} | all-to-all | bytes 1179648 | tf_op jit(solution)/shard_map/all_to_all | solution.py:14
  414.6 31.9 %all-gather.17.cloned.1.call-done = bf16[1,1024,1152]{1,2,0:T(8,128)(2,1)} async-done(((bf16[1,1024,288]{1,2,0:T(8,128)(2,1)}), bf16[1,1024,1152]{1,2,0:T(8,128)(2,1)}) %all-gather.17.cloned.1.call-update) | async-done | bytes 2359312 | tf_op jit(solution)/shard_map/all_gather | solution.py:10
  450.9 5.3 copy.141
  458.9 8.1 %fusion.124 = f32[4,1024,1024]{1,2,0:T(8,128)} fusion(bf16[1024,4,72]{0,2,1:T(8,128)(2,1)S(1)} %bitcast.273, bf16[1024,4,72]{0,2,1:T(8,128)(2,1)S(1)} %bitcast.267), kind=kOutput, calls=%fused_computation.184 | convolution fusion | flops 603979776 | bytes 17956864 | tf_op jit(solution)/shard_map/lbhd,mbhd->bhlm/dot_general | solution.py:53
  467.0 23.1 %fusion.58 = bf16[4,72,1024]{2,1,0:T(8,128)(2,1)} fusion(bf16[1024,4,72]{0,2,1:T(8,128)(2,1)S(1)} %bitcast.278, f32[4,1024,1024]{1,2,0:T(8,128)} %fusion.124, f32[4,1024,1024]{1,2,0:T(8,128)} %get-tuple-element.71, f32[4,1024]{1,0:T(4,128)S(1)} %get-tuple-element.70), kind=kOutput, calls=%fused_computation.90 | convolution fusion | flops 633639936 | bytes 34750464 | tf_op jit(solution)/shard_map/bhlm,mbhd->lbhd/dot_general | solution.py:60
  490.2 22.3 %fusion.61 = bf16[4,72,1024]{2,1,0:T(8,128)(2,1)S(1)} fusion(bf16[1024,4,72]{0,2,1:T(8,128)(2,1)S(1)} %bitcast.276, f32[4,1024,1024]{1,2,0:T(8,128)} %fusion.124, f32[4,1024,1024]{1,2,0:T(8,128)} %get-tuple-element.71, f32[4,1024]{1,0:T(4,128)S(1)} %get-tuple-element.70), kind=kOutput, calls=%fused_computation.91 | convolution fusion | flops 633639936 | bytes 34750464 | tf_op jit(solution)/shard_map/bhlm,lbhd->mbhd/dot_general | solution.py:63
  513.1 8.8 %fusion.67 = bf16[4,72,1024]{2,1,0:T(8,128)(2,1)S(1)} fusion(bf16[1024,4,72]{0,2,1:T(8,128)(2,1)S(1)} %bitcast.274, f32[4,1024,1024]{1,2,0:T(8,128)} %get-tuple-element.71, f32[4,1024]{1,0:T(4,128)S(1)} %get-tuple-element.70), kind=kOutput, calls=%fused_computation.93 | convolution fusion | flops 612663296 | bytes 17973248 | tf_op jit(solution)/shard_map/bhlm,lbhd->mbhd/dot_general | solution.py:47
  537.2 18.5 %reduce-scatter.14.cloned.1.call-done = bf16[144,1152]{1,0:T(8,128)(2,1)} async-done(((bf16[1152,1152]{1,0:T(8,128)(2,1)}), bf16[144,1152]{1,0:T(8,128)(2,1)}) %reduce-scatter.14.cloned.1.call-update) | async-done | bytes 331792 | tf_op jit(solution)/shard_map/reduce_scatter | solution.py:216
  563.2 7.3 %copy.144 = bf16[1152,4,288]{2,1,0:T(4,128)(2,1)} copy(bf16[1152,4,288]{0,2,1:T(8,128)(2,1)} %pad_maximum_fusion.1) | data formatting | bytes 5308416 | tf_op jit(solution)/shard_map/concatenate | solution.py:105
  570.5 6.4 %convert_element_type.247 = bf16[8,144,1152]{2,1,0:T(8,128)(2,1)} reshape(bf16[1152,4,288]{2,1,0:T(4,128)(2,1)} %copy.144) | data formatting | bytes 5308416 | tf_op jit(solution)/shard_map/convert_element_type | solution.py:105
  576.9 36.3 %all_to_all.25 = bf16[8,144,1152]{2,1,0:T(8,128)(2,1)S(1)} all-to-all(bf16[8,144,1152]{2,1,0:T(8,128)(2,1)} %convert_element_type.247), channel_id=1, replica_groups=mesh['heads'=4,'seq'=8] {'seq'}, dimensions={0} | all-to-all | bytes 5308416 | tf_op jit(solution)/shard_map/all_to_all | solution.py:136
  (216 shorter events, 186.9 us)
Async XLA Ops:
  7.2 240.2 %copy-start = (bf16[3,1152,288]{1,2,0:T(8,128)(2,1)S(1)}, bf16[3,1152,288]{1,2,0:T(8,128)(2,1)}, u32[]{:S(2)}) copy-start(bf16[3,1152,288]{1,2,0:T(8,128)(2,1)} %param.11) | copy-start | bytes 5971972
  7.2 55.6 %all-gather.13.cloned.1.call-start = ((), (), s32[]{:S(2)}) async-start(), calls=%async_computation.11 | async-start | bytes 2949120 | tf_op jit(solution)/shard_map/all_gather | solution.py:10
  7.9 92.7 %all-gather.9.cloned.1.call-start = ((), (), s32[]{:S(2)}) async-start(), calls=%async_computation.8 | async-start | bytes 1474560 | tf_op jit(solution)/shard_map/all_gather | solution.py:10
  71.2 81.0 %reduce-scatter.16.cloned.1.call-start = ((), (), s32[]{:S(2)}) async-start(), calls=%async_computation.14 | async-start | bytes 2949120
  77.3 11.9 %copy-start.12 = (bf16[1,1024,288]{1,2,0:T(8,128)(2,1)}, bf16[1,1024,288]{1,2,0:T(8,128)(2,1)S(1)}, u32[]{:S(2)}) copy-start(bf16[1,1024,288]{1,2,0:T(8,128)(2,1)S(1)} %get-tuple-element.64) | copy-start | bytes 1769476
  104.9 89.8 %all-gather.11.cloned.1.call-start = ((), (), s32[]{:S(2)}) async-start(), calls=%async_computation.9 | async-start | bytes 1474560 | tf_op jit(solution)/shard_map/all_gather | solution.py:10
  106.6 53.7 %copy-start.10 = (bf16[1,1024,288]{2,1,0:T(8,128)(2,1)}, bf16[1,1024,288]{2,1,0:T(8,128)(2,1)S(1)}, u32[]{:S(2)}) copy-start(bf16[1,1024,288]{2,1,0:T(8,128)(2,1)S(1)} %copy.110) | copy-start | bytes 1769476
  156.7 83.2 %all-gather.15.cloned.1.call-start = ((), (), s32[]{:S(2)}) async-start(), calls=%async_computation.12 | async-start | bytes 2949120 | tf_op jit(solution)/shard_map/all_gather | solution.py:10
  183.3 8.4 %copy-start.21 = (s32[8,8,8]{2,1,0:T(8,128)S(1)}, s32[8,8,8]{2,1,0:T(8,128)}, u32[]{:S(2)}) copy-start(s32[8,8,8]{2,1,0:T(8,128)} %param.14) | copy-start | bytes 6148
  191.6 173.8 %reduce-scatter.18.cloned.1.call-start = ((), (), s32[]{:S(2)}) async-start(), calls=%async_computation.15 | async-start | bytes 3112960 | tf_op jit(solution)/shard_map/reduce_scatter | solution.py:122
  271.5 10.0 %copy-start.36 = (f32[128,4,8]{2,1,0:T(4,128)}, f32[128,4,8]{2,1,0:T(4,128)S(1)}, u32[]{:S(2)}) copy-start(f32[128,4,8]{2,1,0:T(4,128)S(1)} %get-tuple-element.72) | copy-start | bytes 49156
  316.3 51.1 %copy-start.9 = (bf16[1,1024,288]{1,2,0:T(8,128)(2,1)S(1)}, bf16[1,1024,288]{1,2,0:T(8,128)(2,1)}, u32[]{:S(2)}) copy-start(bf16[1,1024,288]{1,2,0:T(8,128)(2,1)} %copy.113) | copy-start | bytes 1769476
  316.3 130.2 %all-gather.17.cloned.1.call-start = ((), (), s32[]{:S(2)}) async-start(), calls=%async_computation.13 | async-start | bytes 2949120 | tf_op jit(solution)/shard_map/all_gather | solution.py:10
  398.1 137.7 %reduce-scatter.20.cloned.1.call-start = ((), (), s32[]{:S(2)}) async-start(), calls=%async_computation.16 | async-start | bytes 2949120
  450.8 104.9 %reduce-scatter.14.cloned.1.call-start = ((), (), s32[]{:S(2)}) async-start(), calls=%async_computation.10 | async-start | bytes 2985984 | tf_op jit(solution)/shard_map/reduce_scatter | solution.py:216
  467.0 23.2 %copy-start.14 = (bf16[1,1024,288]{1,2,0:T(8,128)(2,1)S(1)}, bf16[1,1024,288]{1,2,0:T(8,128)(2,1)}, u32[]{:S(2)}) copy-start(bf16[1,1024,288]{1,2,0:T(8,128)(2,1)} %get-tuple-element.65) | copy-start | bytes 1769476
  512.5 9.4 %copy-start.32 = (bf16[4,72,1024]{2,1,0:T(8,128)(2,1)}, bf16[4,72,1024]{2,1,0:T(8,128)(2,1)S(1)}, u32[]{:S(2)}) copy-start(bf16[4,72,1024]{2,1,0:T(8,128)(2,1)S(1)} %fusion.61) | copy-start | bytes 1769476
  512.5 9.4 %copy-start.20 = (f32[1024]{0:T(1024)S(1)}, f32[1024]{0:T(1024)}, u32[]{:S(2)}) copy-start(f32[1024]{0:T(1024)} %copy-done.19) | copy-start | bytes 12292
  512.6 9.4 %copy-start.23 = (f32[1024]{0:T(1024)S(1)}, f32[1024]{0:T(1024)}, u32[]{:S(2)}) copy-start(f32[1024]{0:T(1024)} %copy-done.22) | copy-start | bytes 12292
  512.6 9.4 %copy-start.30 = (bf16[4,72,1024]{2,1,0:T(8,128)(2,1)S(1)}, bf16[4,72,1024]{2,1,0:T(8,128)(2,1)}, u32[]{:S(2)}) copy-start(bf16[4,72,1024]{2,1,0:T(8,128)(2,1)} %fusion.58) | copy-start | bytes 1769476
  512.6 107.1 %reduce-scatter.22.cloned.1.call-start = ((), (), s32[]{:S(2)}) async-start(), calls=%async_computation.17 | async-start | bytes 3112960
  513.0 8.9 %copy-start.3 = (bf16[1,1024,1152]{2,1,0:T(8,128)(2,1)S(1)}, bf16[1,1024,1152]{2,1,0:T(8,128)(2,1)}, u32[]{:S(2)}) copy-start(bf16[1,1024,1152]{2,1,0:T(8,128)(2,1)} %copy.108) | copy-start | bytes 7077892
  513.0 8.9 %copy-start.24 = (bf16[3,1152,288]{1,2,0:T(8,128)(2,1)S(1)}, bf16[3,1152,288]{1,2,0:T(8,128)(2,1)}, u32[]{:S(2)}) copy-start(bf16[3,1152,288]{1,2,0:T(8,128)(2,1)} %param.9) | copy-start | bytes 5971972
  535.8 19.9 %copy-start.29 = (bf16[4,72,1024]{2,1,0:T(8,128)(2,1)S(1)}, bf16[4,72,1024]{2,1,0:T(8,128)(2,1)}, u32[]{:S(2)}) copy-start(bf16[4,72,1024]{2,1,0:T(8,128)(2,1)} %copy-done.28) | copy-start | bytes 1769476
  (24 other events, 86.3 us)
Sparse Core Ops, SparseCore 0:
  9.6 53.1 all-gather.12
  71.3 29.2 all-gather.8
  105.0 47.1 reduce-scatter.15
  156.8 29.9 all-gather.10
  191.7 48.1 all-gather.14
  316.4 48.8 reduce-scatter.17
  398.3 48.2 all-gather.16
  451.0 46.8 reduce-scatter.19
  512.7 42.9 reduce-scatter.13
  558.0 50.0 reduce-scatter.21

commit v3 on v2

--- a/solution.py
+++ b/solution.py
@@ -57,6 +57,8 @@
     score_gradient = (
         softmax_weights * (probability_gradient - row_delta) * HEAD_SIZE ** (-0.5)
     ).astype(jnp.bfloat16)
+    if query_rows.shape[1] == 1:
+        score_gradient = lax.optimization_barrier(score_gradient)
     query_gradient = jnp.einsum(
         "bhlm,mbhd->lbhd", score_gradient, key_matrix, preferred_element_type=jnp.float32
     ).astype(jnp.bfloat16)
@@ -207,13 +209,12 @@
         temporal_allowed,
         temporal_state,
     )
+    temporal_sums = exchange_grads(temporal_grads)
+    grad_position, temporal_sums = lax.optimization_barrier((grad_position, temporal_sums))
     hidden_grad = relayout(grad_position.reshape(1, length, own_width)).reshape(length, own_width)
     hidden_grad_rows = row_features(hidden_grad)
-    late_update, temporal_grads, hidden_grad_rows = lax.optimization_barrier(
-        (late_update, temporal_grads, hidden_grad_rows)
-    )
+    late_update, hidden_grad_rows = lax.optimization_barrier((late_update, hidden_grad_rows))
     result = add_update(position_share, late_update)
-    temporal_sums = lax.psum_scatter(temporal_grads, "seq", scatter_dimension=0, tiled=True)
     frames_grad, spatial_grads, early = layer_backward(
         frame_share,
         hidden_grad,
@@ -222,11 +223,11 @@
         out_spatial,
         spatial_allowed,
         spatial_state,
-        (result, temporal_sums),
-    )
-    result, temporal_sums = early
+        result,
+    )
+    result = early
     reduced = split_grads(exchange_grads(spatial_grads), own_width) + split_grads(
-        temporal_sums.astype(jnp.float32), own_width
+        temporal_sums, own_width
     )
     return (
         result.reshape(frame_count, local_count, own_width),

time: 645 us -> 618 us (0.958)
  matrix products: 148 us -> 108 us
  waiting for transfers between devices: 234 us -> 208 us
  other arithmetic: 41.4 us -> 66.5 us
  local copies, waits for them, and re-layouts: 130 us -> 141 us
    reduce_scatter x1, waiting for transfers between devices: 49 us -> 0.01 us  [layer_backward(): summed = lax.psum_scatter(packed, 'heads', scatter_dimension=0, tiled=True)]
    all_to_all x0 -> x1, waiting for transfers between devices: none -> 30.1 us  [exchange_grads(): lax.all_to_all(blocks, 'seq', split_axis=0, concat_axis=0, tiled=True)]
    sub x0 -> x1, other arithmetic: none -> 22.3 us  [attend_backward(): probability_gradient - row_delta]
    dot_general x2, matrix products: 29.4 us -> 7.82 us  [attend_backward(): jnp.einsum('bhlm,mbhd->lbhd', score_gradient, key_matrix, preferred_eleme...]
    dot_general x2, matrix products: 28.5 us -> 8.84 us  [attend_backward(): jnp.einsum('bhlm,lbhd->mbhd', score_gradient, query_rows, preferred_eleme...]
    reduce_scatter x1 -> x0, waiting for transfers between devices: 18.5 us -> none  [shards(): lax.psum_scatter(temporal_grads, 'seq', scatter_dimension=0, tiled=True)]
    all_gather x5, waiting for transfers between devices: 120 us -> 132 us  [row_features(): return lax.all_gather(share_rows, 'heads', axis=1, tiled=True)]
    concatenate x1 -> x2, local copies, waits for them, and re-layouts: 7.35 us -> 14.6 us  [layer_backward(): jnp.concatenate([qkv_grad, out_grad[:, None]], axis=1).astype(jnp.bfloat16)]
  transfers between devices with their start and end apart: 10 -> 10, of which waited for: 7 -> 6; matrix products, arithmetic and copies ran while one was open for 31% -> 31% of each run, Pallas kernels for 0% -> 0%
where the time goes in v3:
time: 618 us; the launch traced here: 607 us
  waiting for transfers between devices  208 us (34%)
  local copies, waits for them, and re-layouts  141 us (23%)
  matrix products  108 us (17%)
  other arithmetic  66.5 us (11%)
  blocking collectives  63.3 us (10%)
  between operations  15.2 us (2%)
    all_gather x5, waiting for transfers between devices, row_features(): return lax.all_gather(share_rows, 'heads', axis=1, tiled=True)  132 us
    unnamed x12, waiting for transfers between devices  46.5 us
    unnamed x104, local copies, waits for them, and re-layouts  42 us
    all_to_all x1, blocking collectives, exchange_grads(): lax.all_to_all(blocks, 'seq', split_axis=0, concat_axis=0, tiled=True)  36.4 us
    all_to_all x1, waiting for transfers between devices, exchange_grads(): lax.all_to_all(blocks, 'seq', split_axis=0, concat_axis=0, tiled=True)  30.1 us
    all_to_all x2, blocking collectives, relayout(): lax.all_to_all(block_rows, 'seq', split_axis=1, concat_axis=0, tiled=True)  26.9 us
    sub x1, other arithmetic, attend_backward(): probability_gradient - row_delta  22.3 us
    sub x2, matrix products, attention_probs(): logit_scores - jnp.max(logit_scores, axis=-1, keepdims=True)  16.5 us
  transfers between devices with their start and end apart: 10, of which 6 were waited for; matrix products, arithmetic and copies ran while one was open for 31% of the time, Pallas kernels for 0%

profile of v3, /device:TPU:0, one launch (start us, length us, event | category | flops | bytes accessed | tf_op | source)
XLA Modules:
  0.0 607.2 jit_solution(11229429832366789778)
XLA Ops:
  12.1 50.7 %all-gather.13.cloned.1.call-done = bf16[1,1024,1152]{1,2,0:T(8,128)(2,1)} async-done(((bf16[1,1024,288]{1,2,0:T(8,128)(2,1)}), bf16[1,1024,1152]{1,2,0:T(8,128)(2,1)}) %all-gather.13.cloned.1.call-update) | async-done | bytes 2359312 | tf_op jit(solution)/shard_map/all_gather | solution.py:10
  71.3 4.9 convert_bitcast_fusion.2
  77.4 11.9 %fusion.117 = (f32[4,1024]{1,0:T(4,128)S(1)}, f32[4,1024,1024]{1,2,0:T(8,128)}) fusion(pred[1024,1024]{0,1:T(8,128)(4,1)} %bitcast_or_fusion, bf16[1024,4,72]{0,2,1:T(8,128)(2,1)} %bitcast.277, bf16[1024,4,72]{0,2,1:T(8,128)(2,1)} %bitcast.275), kind=kOutput, calls=%fused_computation.179 | convolution fusion | flops 620758016 | bytes 19021824 | tf_op jit(solution)/shard_map/sub | solution.py:30
  89.2 7.6 %fusion.65 = bf16[4,72,1024]{2,1,0:T(8,128)(2,1)S(1)} fusion(bf16[1024,4,72]{0,2,1:T(8,128)(2,1)S(1)} %bitcast.272, f32[4,1024,1024]{1,2,0:T(8,128)} %get-tuple-element.71, f32[4,1024]{1,0:T(4,128)S(1)} %get-tuple-element.70), kind=kOutput, calls=%fused_computation.96 | convolution fusion | flops 612663296 | bytes 17973248 | tf_op jit(solution)/shard_map/bhlm,mbhd->lbhd/dot_general | solution.py:36
  106.6 45.7 %reduce-scatter.13.cloned.1.call-done = bf16[288,1024]{1,0:T(8,128)(2,1)} async-done(((bf16[1152,1024]{1,0:T(8,128)(2,1)}), bf16[288,1024]{1,0:T(8,128)(2,1)}) %reduce-scatter.13.cloned.1.call-update) | async-done | bytes 589840
  160.8 6.6 %reduce.15 = bf16[1024,288]{1,0:T(8,128)(2,1)S(1)} reduce(bf16[1024,1,288]{2,1,0:T(2,128)(2,1)} %bitcast.268, bf16[]{:T(256)} %broadcast.328), dimensions={1}, to_apply=%bitcast.254.reduce_sub_computation | reduce | bytes 1179650
  169.3 14.1 %all_to_all.28 = bf16[8,2,18432]{2,1,0:T(2,128)(2,1)S(1)} all-to-all(bf16[8,2,18432]{2,1,0:T(2,128)(2,1)} %reshape.456), channel_id=1, replica_groups=mesh['heads'=4,'seq'=8] {'seq'}, dimensions={0} | all-to-all | bytes 1179648 | tf_op jit(solution)/shard_map/all_to_all | solution.py:14
  187.1 4.6 copy.113
  202.4 37.6 %all-gather.15.cloned.1.call-done = bf16[1,1024,1152]{1,2,0:T(8,128)(2,1)} async-done(((bf16[1,1024,288]{1,2,0:T(8,128)(2,1)}), bf16[1,1024,1152]{1,2,0:T(8,128)(2,1)}) %all-gather.15.cloned.1.call-update) | async-done | bytes 2359312 | tf_op jit(solution)/shard_map/all_gather | solution.py:10
  266.9 4.6 fusion.118
  275.3 6.2 %fusion.56 = bf16[8,128,4,72]{3,0,2,1:T(8,128)(2,1)} fusion(bf16[8,128,4,72]{3,0,2,1:T(8,128)(2,1)} %copy.117, f32[128,4,8,8]{2,3,1,0:T(8,128)} %fusion.119, f32[128,4,8,8]{2,3,1,0:T(8,128)} %get-tuple-element.73, f32[128,4,8]{2,1,0:T(4,128)S(1)} %get-tuple-element.72), kind=kOutput, calls=%fused_computation.91 | convolution fusion | flops 5246983 | bytes 1458176 | tf_op jit(solution)/shard_map/bhlm,mbhd->lbhd/dot_general | solution.py:62
  281.5 6.2 %fusion.57 = bf16[8,128,4,72]{3,0,2,1:T(8,128)(2,1)} fusion(bf16[8,128,4,72]{3,0,2,1:T(8,128)(2,1)} %copy.116, f32[128,4,8,8]{2,3,1,0:T(8,128)} %fusion.119, f32[128,4,8,8]{2,3,1,0:T(8,128)} %get-tuple-element.73, f32[128,4,8]{2,1,0:T(4,128)S(1)} %get-tuple-element.72), kind=kOutput, calls=%fused_computation.92 | convolution fusion | flops 5246983 | bytes 1458176 | tf_op jit(solution)/shard_map/bhlm,lbhd->mbhd/dot_general | solution.py:65
  331.1 7.3 %copy.134 = bf16[1152,4,288]{2,1,0:T(4,128)(2,1)} copy(bf16[1152,4,288]{0,2,1:T(8,128)(2,1)} %pad_maximum_fusion) | data formatting | bytes 5308416 | tf_op jit(solution)/shard_map/concatenate | solution.py:107
  338.4 6.4 %convert_element_type.231 = bf16[8,144,1152]{2,1,0:T(8,128)(2,1)} reshape(bf16[1152,4,288]{2,1,0:T(4,128)(2,1)} %copy.134) | data formatting | bytes 5308416 | tf_op jit(solution)/shard_map/convert_element_type | solution.py:107
  344.8 36.4 %all_to_all.29 = bf16[8,144,1152]{2,1,0:T(8,128)(2,1)S(1)} all-to-all(bf16[8,144,1152]{2,1,0:T(8,128)(2,1)} %convert_element_type.231), channel_id=1, replica_groups=mesh['heads'=4,'seq'=8] {'seq'}, dimensions={0} | all-to-all | bytes 5308416 | tf_op jit(solution)/shard_map/all_to_all | solution.py:138
  389.7 5.7 reduce.16
  396.5 12.8 %all_to_all.30 = bf16[8,2,18432]{2,1,0:T(2,128)(2,1)S(1)} all-to-all(bf16[8,2,18432]{2,1,0:T(2,128)(2,1)S(1)} %reshape.458), channel_id=1, replica_groups=mesh['heads'=4,'seq'=8] {'seq'}, dimensions={0} | all-to-all | bytes 1179648 | tf_op jit(solution)/shard_map/all_to_all | solution.py:14
  418.2 43.6 %all-gather.17.cloned.1.call-done = bf16[1,1024,1152]{1,2,0:T(8,128)(2,1)} async-done(((bf16[1,1024,288]{1,2,0:T(8,128)(2,1)}), bf16[1,1024,1152]{1,2,0:T(8,128)(2,1)}) %all-gather.17.cloned.1.call-update) | async-done | bytes 2359312 | tf_op jit(solution)/shard_map/all_gather | solution.py:10
  469.9 8.1 %fusion.120 = f32[4,1024,1024]{1,2,0:T(8,128)} fusion(bf16[1024,4,72]{0,2,1:T(8,128)(2,1)S(1)} %bitcast.284, bf16[1024,4,72]{0,2,1:T(8,128)(2,1)S(1)} %bitcast.273), kind=kOutput, calls=%fused_computation.183 | convolution fusion | flops 603979776 | bytes 17956864 | tf_op jit(solution)/shard_map/lbhd,mbhd->bhlm/dot_general | solution.py:53
  478.0 22.3 %fusion.17 = bf16[1,4,1024,1024]{2,3,1,0:T(8,128)(2,1)S(1)} fusion(f32[4,1024,1024]{1,2,0:T(8,128)} %fusion.120, f32[4,1024,1024]{1,2,0:T(8,128)} %get-tuple-element.71, f32[4,1024]{1,0:T(4,128)S(1)} %get-tuple-element.70), kind=kOutput, calls=%fused_computation.24 | output fusion | flops 29365248 | bytes 41959424 | tf_op jit(solution)/shard_map/sub | solution.py:58
  504.7 8.8 %fusion.68 = bf16[4,72,1024]{2,1,0:T(8,128)(2,1)S(1)} fusion(bf16[1024,4,72]{0,2,1:T(8,128)(2,1)S(1)} %bitcast.285, f32[4,1024,1024]{1,2,0:T(8,128)} %get-tuple-element.71, f32[4,1024]{1,0:T(4,128)S(1)} %get-tuple-element.70), kind=kOutput, calls=%fused_computation.97 | convolution fusion | flops 612663296 | bytes 17973248 | tf_op jit(solution)/shard_map/bhlm,lbhd->mbhd/dot_general | solution.py:47
  536.1 7.3 %copy.144 = bf16[1152,4,288]{2,1,0:T(4,128)(2,1)} copy(bf16[1152,4,288]{0,2,1:T(8,128)(2,1)} %pad_maximum_fusion.1) | data formatting | bytes 5308416 | tf_op jit(solution)/shard_map/concatenate | solution.py:107
  543.4 6.4 %convert_element_type.253 = bf16[8,144,1152]{2,1,0:T(8,128)(2,1)} reshape(bf16[1152,4,288]{2,1,0:T(4,128)(2,1)} %copy.144) | data formatting | bytes 5308416 | tf_op jit(solution)/shard_map/convert_element_type | solution.py:107
  556.9 30.1 %all-to-all-done.3 = bf16[8,144,1152]{2,1,0:T(8,128)(2,1)} async-done(((bf16[8,144,1152]{2,1,0:T(8,128)(2,1)}), bf16[8,144,1152]{2,1,0:T(8,128)(2,1)}, u32[]{:S(2)}, u32[]{:S(2)}) %all-to-all-start.3) | async-done | bytes 2654240 | tf_op jit(solution)/shard_map/all_to_all | solution.py:138
  (222 shorter events, 196.4 us)
Async XLA Ops:
  7.2 240.3 %copy-start = (bf16[3,1152,288]{1,2,0:T(8,128)(2,1)S(1)}, bf16[3,1152,288]{1,2,0:T(8,128)(2,1)}, u32[]{:S(2)}) copy-start(bf16[3,1152,288]{1,2,0:T(8,128)(2,1)} %param.11) | copy-start | bytes 5971972
  7.2 55.6 %all-gather.13.cloned.1.call-start = ((), (), s32[]{:S(2)}) async-start(), calls=%async_computation.10 | async-start | bytes 2949120 | tf_op jit(solution)/shard_map/all_gather | solution.py:10
  7.9 92.7 %all-gather.9.cloned.1.call-start = ((), (), s32[]{:S(2)}) async-start(), calls=%async_computation.8 | async-start | bytes 1474560 | tf_op jit(solution)/shard_map/all_gather | solution.py:10
  71.2 81.0 %reduce-scatter.13.cloned.1.call-start = ((), (), s32[]{:S(2)}) async-start(), calls=%async_computation.13 | async-start | bytes 2949120
  77.4 11.9 %copy-start.13 = (bf16[1,1024,288]{1,2,0:T(8,128)(2,1)}, bf16[1,1024,288]{1,2,0:T(8,128)(2,1)S(1)}, u32[]{:S(2)}) copy-start(bf16[1,1024,288]{1,2,0:T(8,128)(2,1)S(1)} %get-tuple-element.64) | copy-start | bytes 1769476
  89.2 8.4 %copy-start.32 = (bf16[288,1152]{1,0:T(8,128)(2,1)S(1)}, bf16[288,1152]{1,0:T(8,128)(2,1)}, u32[]{:S(2)}) copy-start(bf16[288,1152]{1,0:T(8,128)(2,1)} %param.10) | copy-start | bytes 1990660
  104.9 89.9 %all-gather.11.cloned.1.call-start = ((), (), s32[]{:S(2)}) async-start(), calls=%async_computation.9 | async-start | bytes 1474560 | tf_op jit(solution)/shard_map/all_gather | solution.py:10
  106.6 53.7 %copy-start.10 = (bf16[1,1024,288]{2,1,0:T(8,128)(2,1)}, bf16[1,1024,288]{2,1,0:T(8,128)(2,1)S(1)}, u32[]{:S(2)}) copy-start(bf16[1,1024,288]{2,1,0:T(8,128)(2,1)S(1)} %copy.110) | copy-start | bytes 1769476
  156.7 83.3 %all-gather.15.cloned.1.call-start = ((), (), s32[]{:S(2)}) async-start(), calls=%async_computation.11 | async-start | bytes 2949120 | tf_op jit(solution)/shard_map/all_gather | solution.py:10
  183.4 8.4 %copy-start.28 = (s32[8,8,8]{2,1,0:T(8,128)S(1)}, s32[8,8,8]{2,1,0:T(8,128)}, u32[]{:S(2)}) copy-start(s32[8,8,8]{2,1,0:T(8,128)} %param.14) | copy-start | bytes 6148
  191.7 190.7 %reduce-scatter.15.cloned.1.call-start = ((), (), s32[]{:S(2)}) async-start(), calls=%async_computation.14 | async-start | bytes 3112960 | tf_op jit(solution)/shard_map/reduce_scatter | solution.py:124
  271.6 9.9 %copy-start.38 = (f32[128,4,8]{2,1,0:T(4,128)}, f32[128,4,8]{2,1,0:T(4,128)S(1)}, u32[]{:S(2)}) copy-start(f32[128,4,8]{2,1,0:T(4,128)S(1)} %get-tuple-element.72) | copy-start | bytes 49156
  316.5 145.3 %all-gather.17.cloned.1.call-start = ((), (), s32[]{:S(2)}) async-start(), calls=%async_computation.12 | async-start | bytes 2949120 | tf_op jit(solution)/shard_map/all_gather | solution.py:10
  410.9 7.3 %copy-start.8 = (bf16[1024,1,288]{2,1,0:T(2,128)(2,1)}, bf16[1024,1,288]{2,1,0:T(2,128)(2,1)S(1)}, u32[]{:S(2)}) copy-start(bf16[1024,1,288]{2,1,0:T(2,128)(2,1)S(1)} %reshape.459) | copy-start | bytes 1769476
  414.2 113.1 %reduce-scatter.17.cloned.1.call-start = ((), (), s32[]{:S(2)}) async-start(), calls=%async_computation.15 | async-start | bytes 2949120
  466.2 126.4 %reduce-scatter.19.cloned.1.call-start = ((), (), s32[]{:S(2)}) async-start(), calls=%async_computation.16 | async-start | bytes 3112960
  478.0 22.4 %copy-start.17 = (bf16[1,1024,288]{1,2,0:T(8,128)(2,1)S(1)}, bf16[1,1024,288]{1,2,0:T(8,128)(2,1)}, u32[]{:S(2)}) copy-start(bf16[1,1024,288]{1,2,0:T(8,128)(2,1)} %get-tuple-element.65) | copy-start | bytes 1769476
  503.0 10.5 %copy-start.18 = (bf16[4,72,1024]{2,1,0:T(8,128)(2,1)}, bf16[4,72,1024]{2,1,0:T(8,128)(2,1)S(1)}, u32[]{:S(2)}) copy-start(bf16[4,72,1024]{2,1,0:T(8,128)(2,1)S(1)} %fusion.62) | copy-start | bytes 1769476
  504.7 8.9 %copy-start.20 = (bf16[4,72,1024]{2,1,0:T(8,128)(2,1)}, bf16[4,72,1024]{2,1,0:T(8,128)(2,1)S(1)}, u32[]{:S(2)}) copy-start(bf16[4,72,1024]{2,1,0:T(8,128)(2,1)S(1)} %fusion.59) | copy-start | bytes 1769476
  504.7 8.9 %copy-start.3 = (bf16[1,1024,1152]{2,1,0:T(8,128)(2,1)S(1)}, bf16[1,1024,1152]{2,1,0:T(8,128)(2,1)}, u32[]{:S(2)}) copy-start(bf16[1,1024,1152]{2,1,0:T(8,128)(2,1)} %copy.108) | copy-start | bytes 7077892
  504.7 8.9 %copy-start.27 = (f32[1024]{0:T(1024)S(1)}, f32[1024]{0:T(1024)}, u32[]{:S(2)}) copy-start(f32[1024]{0:T(1024)} %copy-done.26) | copy-start | bytes 12292
  504.7 8.8 %copy-start.30 = (f32[1024]{0:T(1024)S(1)}, f32[1024]{0:T(1024)}, u32[]{:S(2)}) copy-start(f32[1024]{0:T(1024)} %copy-done.29) | copy-start | bytes 12292
  504.7 8.8 %copy-start.31 = (bf16[3,1152,288]{1,2,0:T(8,128)(2,1)S(1)}, bf16[3,1152,288]{1,2,0:T(8,128)(2,1)}, u32[]{:S(2)}) copy-start(bf16[3,1152,288]{1,2,0:T(8,128)(2,1)} %param.9) | copy-start | bytes 5971972
  549.8 37.2 %all-to-all-start.3 = ((bf16[8,144,1152]{2,1,0:T(8,128)(2,1)}), bf16[8,144,1152]{2,1,0:T(8,128)(2,1)}, u32[]{:S(2)}, u32[]{:S(2)}) async-start(bf16[8,144,1152]{2,1,0:T(8,128)(2,1)} %convert_element_type.253), calls=%async_computation.3 | async-start | bytes 5308416 | tf_op jit(solution)/shard_map/all_to_all | solution.py:138
  (26 other events, 70.5 us)
Sparse Core Ops, SparseCore 0:
  9.6 53.1 all-gather.12
  71.3 29.2 all-gather.8
  105.0 47.1 reduce-scatter.12
  156.8 29.9 all-gather.10
  191.8 48.1 all-gather.14
  316.6 48.8 reduce-scatter.14
  414.3 47.4 all-gather.16
  466.3 46.8 reduce-scatter.16
  528.8 48.9 reduce-scatter.18

commit v4 on v3

--- a/solution.py
+++ b/solution.py
@@ -103,9 +103,12 @@
         shaped[0], shaped[1], shaped[2], allowed, grad_mixed
     )
     qkv_grads = jnp.stack([query_gradient, key_gradient, value_gradient]).reshape(3, -1, own_width)
-    qkv_grad = jnp.einsum("nd,kne->dke", normed_low, qkv_grads, preferred_element_type=jnp.float32)
-    weight_grads = jnp.concatenate([qkv_grad, out_grad[:, None]], axis=1).astype(jnp.bfloat16)
-    weight_grads = weight_grads.reshape(-1, 4 * own_width)
+    qkv_grad = [
+        jnp.einsum("nd,ne->de", normed_low, part, preferred_element_type=jnp.float32)
+        for part in qkv_grads
+    ]
+    parts = qkv_grad + [out_grad]
+    weight_grads = jnp.concatenate([part.astype(jnp.bfloat16) for part in parts], axis=1)
     partial_term = jnp.einsum(
         "kne,kde->dn", qkv_grads, qkv_weights, preferred_element_type=jnp.float32
     )

time: 618 us -> 610 us (0.987)
  local copies, waits for them, and re-layouts: 141 us -> 122 us
  other arithmetic: 66.5 us -> 77.9 us
    convert_element_type x2 -> x0, local copies, waits for them, and re-layouts: 12.8 us -> none  [layer_backward(): jnp.concatenate([qkv_grad, out_grad[:, None]], axis=1).astype(jnp.bfloat16)]
    concatenate x2, other arithmetic: 3.55 us -> 11.8 us  [layer_backward(): jnp.concatenate([part.astype(jnp.bfloat16) for part in parts], axis=1)]
    unnamed x104 -> x106, local copies, waits for them, and re-layouts: 42 us -> 39.7 us
  transfers between devices with their start and end apart: 10 -> 10, of which waited for: 6 -> 5; matrix products, arithmetic and copies ran while one was open for 31% -> 30% of each run, Pallas kernels for 0% -> 0%
where the time goes in v4:
time: 610 us; the launch traced here: 599 us
  waiting for transfers between devices  208 us (34%)
  local copies, waits for them, and re-layouts  122 us (20%)
  matrix products  107 us (18%)
  other arithmetic  77.9 us (13%)
  blocking collectives  63.3 us (10%)
  between operations  15 us (2%)
    all_gather x5, waiting for transfers between devices, row_features(): return lax.all_gather(share_rows, 'heads', axis=1, tiled=True)  132 us
    unnamed x12, waiting for transfers between devices  46.4 us
    unnamed x106, local copies, waits for them, and re-layouts  39.7 us
    all_to_all x1, blocking collectives, exchange_grads(): lax.all_to_all(blocks, 'seq', split_axis=0, concat_axis=0, tiled=True)  36.5 us
    all_to_all x1, waiting for transfers between devices, exchange_grads(): lax.all_to_all(blocks, 'seq', split_axis=0, concat_axis=0, tiled=True)  30.1 us
    all_to_all x2, blocking collectives, relayout(): lax.all_to_all(block_rows, 'seq', split_axis=1, concat_axis=0, tiled=True)  26.9 us
    sub x1, other arithmetic, attend_backward(): probability_gradient - row_delta  22.3 us
    sub x2, matrix products, attention_probs(): logit_scores - jnp.max(logit_scores, axis=-1, keepdims=True)  16.5 us
  transfers between devices with their start and end apart: 10, of which 5 were waited for; matrix products, arithmetic and copies ran while one was open for 30% of the time, Pallas kernels for 0%

profile of v4, /device:TPU:0, one launch (start us, length us, event | category | flops | bytes accessed | tf_op | source)
XLA Modules:
  0.0 598.6 jit_solution(2463540032215650919)
XLA Ops:
  12.1 50.7 %all-gather.13.cloned.1.call-done = bf16[1,1024,1152]{1,2,0:T(8,128)(2,1)} async-done(((bf16[1,1024,288]{1,2,0:T(8,128)(2,1)}), bf16[1,1024,1152]{1,2,0:T(8,128)(2,1)}) %all-gather.13.cloned.1.call-update) | async-done | bytes 2359312 | tf_op jit(solution)/shard_map/all_gather | solution.py:10
  77.3 11.9 %fusion.134 = (f32[4,1024]{1,0:T(4,128)S(1)}, f32[4,1024,1024]{1,2,0:T(8,128)}) fusion(pred[1024,1024]{0,1:T(8,128)(4,1)} %bitcast_or_fusion, bf16[1024,4,72]{0,2,1:T(8,128)(2,1)} %bitcast.308, bf16[1024,4,72]{0,2,1:T(8,128)(2,1)} %bitcast.306), kind=kOutput, calls=%fused_computation.196 | convolution fusion | flops 620758016 | bytes 19021824 | tf_op jit(solution)/shard_map/sub | solution.py:30
  89.2 7.6 %fusion.81 = bf16[4,72,1024]{2,1,0:T(8,128)(2,1)S(1)} fusion(bf16[1024,4,72]{0,2,1:T(8,128)(2,1)S(1)} %bitcast.303, f32[4,1024,1024]{1,2,0:T(8,128)} %get-tuple-element.71, f32[4,1024]{1,0:T(4,128)S(1)} %get-tuple-element.70), kind=kOutput, calls=%fused_computation.111 | convolution fusion | flops 612663296 | bytes 17973248 | tf_op jit(solution)/shard_map/bhlm,mbhd->lbhd/dot_general | solution.py:36
  106.6 45.6 %reduce-scatter.13.cloned.1.call-done = bf16[288,1024]{1,0:T(8,128)(2,1)} async-done(((bf16[1152,1024]{1,0:T(8,128)(2,1)}), bf16[288,1024]{1,0:T(8,128)(2,1)}) %reduce-scatter.13.cloned.1.call-update) | async-done | bytes 589840
  160.8 6.6 %reduce.15 = bf16[1024,288]{1,0:T(8,128)(2,1)S(1)} reduce(bf16[1024,1,288]{2,1,0:T(2,128)(2,1)} %bitcast.299, bf16[]{:T(256)} %broadcast.328), dimensions={1}, to_apply=%bitcast.284.reduce_sub_computation | reduce | bytes 1179650
  169.4 14.1 %all_to_all.28 = bf16[8,2,18432]{2,1,0:T(2,128)(2,1)S(1)} all-to-all(bf16[8,2,18432]{2,1,0:T(2,128)(2,1)} %reshape.478), channel_id=1, replica_groups=mesh['heads'=4,'seq'=8] {'seq'}, dimensions={0} | all-to-all | bytes 1179648 | tf_op jit(solution)/shard_map/all_to_all | solution.py:14
  187.1 4.6 copy.119
  202.6 37.4 %all-gather.15.cloned.1.call-done = bf16[1,1024,1152]{1,2,0:T(8,128)(2,1)} async-done(((bf16[1,1024,288]{1,2,0:T(8,128)(2,1)}), bf16[1,1024,1152]{1,2,0:T(8,128)(2,1)}) %all-gather.15.cloned.1.call-update) | async-done | bytes 2359312 | tf_op jit(solution)/shard_map/all_gather | solution.py:10
  267.5 4.6 fusion.135
  275.8 6.2 %fusion.72 = bf16[8,128,4,72]{3,0,2,1:T(8,128)(2,1)} fusion(bf16[8,128,4,72]{3,0,2,1:T(8,128)(2,1)} %copy.123, f32[128,4,8,8]{2,3,1,0:T(8,128)} %fusion.136, f32[128,4,8,8]{2,3,1,0:T(8,128)} %get-tuple-element.73, f32[128,4,8]{2,1,0:T(4,128)S(1)} %get-tuple-element.72), kind=kOutput, calls=%fused_computation.106 | convolution fusion | flops 5246983 | bytes 1458176 | tf_op jit(solution)/shard_map/bhlm,mbhd->lbhd/dot_general | solution.py:62
  282.0 6.1 %fusion.73 = bf16[8,128,4,72]{3,0,2,1:T(8,128)(2,1)} fusion(bf16[8,128,4,72]{3,0,2,1:T(8,128)(2,1)} %copy.122, f32[128,4,8,8]{2,3,1,0:T(8,128)} %fusion.136, f32[128,4,8,8]{2,3,1,0:T(8,128)} %get-tuple-element.73, f32[128,4,8]{2,1,0:T(4,128)S(1)} %get-tuple-element.72), kind=kOutput, calls=%fused_computation.107 | convolution fusion | flops 5246983 | bytes 1458176 | tf_op jit(solution)/shard_map/bhlm,lbhd->mbhd/dot_general | solution.py:65
  301.2 6.0 bitcast_reduce_fusion.1
  329.4 5.9 pad_maximum_fusion
  335.3 5.2 copy.143
  340.6 36.5 %all_to_all.29 = bf16[8,144,1152]{2,1,0:T(8,128)(2,1)S(1)} all-to-all(bf16[8,144,1152]{2,1,0:T(8,128)(2,1)} %bitcast.292), channel_id=1, replica_groups=mesh['heads'=4,'seq'=8] {'seq'}, dimensions={0} | all-to-all | bytes 5308416 | tf_op jit(solution)/shard_map/all_to_all | solution.py:141
  385.5 5.7 reduce.16
  392.3 12.8 %all_to_all.30 = bf16[8,2,18432]{2,1,0:T(2,128)(2,1)S(1)} all-to-all(bf16[8,2,18432]{2,1,0:T(2,128)(2,1)S(1)} %reshape.480), channel_id=1, replica_groups=mesh['heads'=4,'seq'=8] {'seq'}, dimensions={0} | all-to-all | bytes 1179648 | tf_op jit(solution)/shard_map/all_to_all | solution.py:14
  414.1 43.5 %all-gather.17.cloned.1.call-done = bf16[1,1024,1152]{1,2,0:T(8,128)(2,1)} async-done(((bf16[1,1024,288]{1,2,0:T(8,128)(2,1)}), bf16[1,1024,1152]{1,2,0:T(8,128)(2,1)}) %all-gather.17.cloned.1.call-update) | async-done | bytes 2359312 | tf_op jit(solution)/shard_map/all_gather | solution.py:10
  465.6 8.1 %fusion.137 = f32[4,1024,1024]{1,2,0:T(8,128)} fusion(bf16[1024,4,72]{0,2,1:T(8,128)(2,1)S(1)} %bitcast.318, bf16[1024,4,72]{0,2,1:T(8,128)(2,1)S(1)} %bitcast.304), kind=kOutput, calls=%fused_computation.200 | convolution fusion | flops 603979776 | bytes 17956864 | tf_op jit(solution)/shard_map/lbhd,mbhd->bhlm/dot_general | solution.py:53
  473.7 22.3 %fusion.17 = bf16[1,4,1024,1024]{2,3,1,0:T(8,128)(2,1)S(1)} fusion(f32[4,1024,1024]{1,2,0:T(8,128)} %fusion.137, f32[4,1024,1024]{1,2,0:T(8,128)} %get-tuple-element.71, f32[4,1024]{1,0:T(4,128)S(1)} %get-tuple-element.70), kind=kOutput, calls=%fused_computation.24 | output fusion | flops 29365248 | bytes 41959424 | tf_op jit(solution)/shard_map/sub | solution.py:58
  500.5 8.8 %fusion.84 = bf16[4,72,1024]{2,1,0:T(8,128)(2,1)S(1)} fusion(bf16[1024,4,72]{0,2,1:T(8,128)(2,1)S(1)} %bitcast.319, f32[4,1024,1024]{1,2,0:T(8,128)} %get-tuple-element.71, f32[4,1024]{1,0:T(4,128)S(1)} %get-tuple-element.70), kind=kOutput, calls=%fused_computation.112 | convolution fusion | flops 612663296 | bytes 17973248 | tf_op jit(solution)/shard_map/bhlm,lbhd->mbhd/dot_general | solution.py:47
  530.3 5.9 pad_maximum_fusion.1
  536.2 5.2 copy.153
  548.5 30.1 %all-to-all-done.3 = bf16[8,144,1152]{2,1,0:T(8,128)(2,1)} async-done(((bf16[8,144,1152]{2,1,0:T(8,128)(2,1)}), bf16[8,144,1152]{2,1,0:T(8,128)(2,1)}, u32[]{:S(2)}, u32[]{:S(2)}) %all-to-all-start.3) | async-done | bytes 2654240 | tf_op jit(solution)/shard_map/all_to_all | solution.py:141
  (227 shorter events, 192.3 us)
Async XLA Ops:
  7.2 241.0 %copy-start = (bf16[3,1152,288]{1,2,0:T(8,128)(2,1)S(1)}, bf16[3,1152,288]{1,2,0:T(8,128)(2,1)}, u32[]{:S(2)}) copy-start(bf16[3,1152,288]{1,2,0:T(8,128)(2,1)} %param.11) | copy-start | bytes 5971972
  7.2 55.6 %all-gather.13.cloned.1.call-start = ((), (), s32[]{:S(2)}) async-start(), calls=%async_computation.10 | async-start | bytes 2949120 | tf_op jit(solution)/shard_map/all_gather | solution.py:10
  7.9 92.6 %all-gather.9.cloned.1.call-start = ((), (), s32[]{:S(2)}) async-start(), calls=%async_computation.8 | async-start | bytes 1474560 | tf_op jit(solution)/shard_map/all_gather | solution.py:10
  71.2 81.0 %reduce-scatter.13.cloned.1.call-start = ((), (), s32[]{:S(2)}) async-start(), calls=%async_computation.13 | async-start | bytes 2949120
  77.3 11.9 %copy-start.10 = (bf16[1,1024,288]{1,2,0:T(8,128)(2,1)}, bf16[1,1024,288]{1,2,0:T(8,128)(2,1)S(1)}, u32[]{:S(2)}) copy-start(bf16[1,1024,288]{1,2,0:T(8,128)(2,1)S(1)} %get-tuple-element.64) | copy-start | bytes 1769476
  89.2 8.4 %copy-start.34 = (bf16[288,1152]{1,0:T(8,128)(2,1)S(1)}, bf16[288,1152]{1,0:T(8,128)(2,1)}, u32[]{:S(2)}) copy-start(bf16[288,1152]{1,0:T(8,128)(2,1)} %param.10) | copy-start | bytes 1990660
  104.9 90.0 %all-gather.11.cloned.1.call-start = ((), (), s32[]{:S(2)}) async-start(), calls=%async_computation.9 | async-start | bytes 1474560 | tf_op jit(solution)/shard_map/all_gather | solution.py:10
  106.6 53.7 %copy-start.7 = (bf16[1,1024,288]{2,1,0:T(8,128)(2,1)}, bf16[1,1024,288]{2,1,0:T(8,128)(2,1)S(1)}, u32[]{:S(2)}) copy-start(bf16[1,1024,288]{2,1,0:T(8,128)(2,1)S(1)} %copy.116) | copy-start | bytes 1769476
  156.7 83.3 %all-gather.15.cloned.1.call-start = ((), (), s32[]{:S(2)}) async-start(), calls=%async_computation.11 | async-start | bytes 2949120 | tf_op jit(solution)/shard_map/all_gather | solution.py:10
  183.4 8.4 %copy-start.31 = (s32[8,8,8]{2,1,0:T(8,128)S(1)}, s32[8,8,8]{2,1,0:T(8,128)}, u32[]{:S(2)}) copy-start(s32[8,8,8]{2,1,0:T(8,128)} %param.14) | copy-start | bytes 6148
  191.7 186.5 %reduce-scatter.15.cloned.1.call-start = ((), (), s32[]{:S(2)}) async-start(), calls=%async_computation.14 | async-start | bytes 3112960 | tf_op jit(solution)/shard_map/reduce_scatter | solution.py:127
  272.1 9.9 %copy-start.40 = (f32[128,4,8]{2,1,0:T(4,128)}, f32[128,4,8]{2,1,0:T(4,128)S(1)}, u32[]{:S(2)}) copy-start(f32[128,4,8]{2,1,0:T(4,128)S(1)} %get-tuple-element.72) | copy-start | bytes 49156
  316.7 140.9 %all-gather.17.cloned.1.call-start = ((), (), s32[]{:S(2)}) async-start(), calls=%async_computation.12 | async-start | bytes 2949120 | tf_op jit(solution)/shard_map/all_gather | solution.py:10
  406.7 7.3 %copy-start.5 = (bf16[1024,1,288]{2,1,0:T(2,128)(2,1)}, bf16[1024,1,288]{2,1,0:T(2,128)(2,1)S(1)}, u32[]{:S(2)}) copy-start(bf16[1024,1,288]{2,1,0:T(2,128)(2,1)S(1)} %reshape.481) | copy-start | bytes 1769476
  410.0 113.0 %reduce-scatter.17.cloned.1.call-start = ((), (), s32[]{:S(2)}) async-start(), calls=%async_computation.15 | async-start | bytes 2949120
  461.9 122.3 %reduce-scatter.19.cloned.1.call-start = ((), (), s32[]{:S(2)}) async-start(), calls=%async_computation.16 | async-start | bytes 3112960
  473.7 22.4 %copy-start.14 = (bf16[1,1024,288]{1,2,0:T(8,128)(2,1)S(1)}, bf16[1,1024,288]{1,2,0:T(8,128)(2,1)}, u32[]{:S(2)}) copy-start(bf16[1,1024,288]{1,2,0:T(8,128)(2,1)} %get-tuple-element.65) | copy-start | bytes 1769476
  498.8 10.5 %copy-start.23 = (bf16[4,72,1024]{2,1,0:T(8,128)(2,1)}, bf16[4,72,1024]{2,1,0:T(8,128)(2,1)S(1)}, u32[]{:S(2)}) copy-start(bf16[4,72,1024]{2,1,0:T(8,128)(2,1)S(1)} %fusion.78) | copy-start | bytes 1769476
  500.4 8.9 %copy-start.21 = (bf16[4,72,1024]{2,1,0:T(8,128)(2,1)}, bf16[4,72,1024]{2,1,0:T(8,128)(2,1)S(1)}, u32[]{:S(2)}) copy-start(bf16[4,72,1024]{2,1,0:T(8,128)(2,1)S(1)} %fusion.75) | copy-start | bytes 1769476
  500.4 8.9 %copy-start.3 = (bf16[1,1024,1152]{2,1,0:T(8,128)(2,1)S(1)}, bf16[1,1024,1152]{2,1,0:T(8,128)(2,1)}, u32[]{:S(2)}) copy-start(bf16[1,1024,1152]{2,1,0:T(8,128)(2,1)} %copy.114) | copy-start | bytes 7077892
  500.4 8.9 %copy-start.28 = (f32[1024]{0:T(1024)S(1)}, f32[1024]{0:T(1024)}, u32[]{:S(2)}) copy-start(f32[1024]{0:T(1024)} %copy-done.27) | copy-start | bytes 12292
  500.4 8.9 %copy-start.30 = (f32[1024]{0:T(1024)S(1)}, f32[1024]{0:T(1024)}, u32[]{:S(2)}) copy-start(f32[1024]{0:T(1024)} %copy-done.29) | copy-start | bytes 12292
  500.4 8.8 %copy-start.33 = (bf16[3,1152,288]{1,2,0:T(8,128)(2,1)S(1)}, bf16[3,1152,288]{1,2,0:T(8,128)(2,1)}, u32[]{:S(2)}) copy-start(bf16[3,1152,288]{1,2,0:T(8,128)(2,1)} %param.9) | copy-start | bytes 5971972
  541.4 37.2 %all-to-all-start.3 = ((bf16[8,144,1152]{2,1,0:T(8,128)(2,1)}), bf16[8,144,1152]{2,1,0:T(8,128)(2,1)}, u32[]{:S(2)}, u32[]{:S(2)}) async-start(bf16[8,144,1152]{2,1,0:T(8,128)(2,1)} %bitcast.291), calls=%async_computation.3 | async-start | bytes 5308416 | tf_op jit(solution)/shard_map/all_to_all | solution.py:141
  (28 other events, 72.4 us)
Sparse Core Ops, SparseCore 0:
  9.6 53.1 all-gather.12
  71.3 29.2 all-gather.8
  105.0 47.1 reduce-scatter.12
  156.8 29.9 all-gather.10
  191.8 48.1 all-gather.14
  316.8 48.8 reduce-scatter.14
  410.1 47.4 all-gather.16
  462.0 46.8 reduce-scatter.16
  524.4 48.9 reduce-scatter.18
